TPU v7x, 32 devices: a whole 2x2x4 slice. The times are simulated.
32 devices in a mesh: groups: 2 (over y), blk: 4 (over z), heads: 2 (over x), section: 2 (over core).
Axes of the slice: x: 2, y: 2, z: 4, core: 2. Of those that a mesh axis runs over, the one named last changes fastest.
Arguments:
- dec_states: bfloat16 [4096, 2304], P(('groups', 'blk', 'section')), parts along dimension 0, may hold values from -6 to 6
- cross_keys: bfloat16 [1024, 1, 256], P(('groups', 'blk')), parts along dimension 0, may hold values from -15 to 15
- cross_values: bfloat16 [1024, 1, 256], P(('groups', 'blk')), parts along dimension 0, may hold values from -6 to 6
- attn_gain: float32 [2304], replicated, may hold values from 0.1 to 1.9
- query_weight: bfloat16 [2304, 512], P(None, 'heads'), may hold values from -0.125 to 0.125
- out_weight: bfloat16 [512, 2304], P('heads'), may hold values from -0.25 to 0.25
- post_attn_gain: float32 [2304], replicated, may hold values from 0.1 to 1.9
- ffn_gain: float32 [2304], replicated, may hold values from 0.1 to 1.9
- gate_weight: bfloat16 [2304, 9216], P('blk', ('heads', 'section')), may hold values from -0.125 to 0.125
- up_weight: bfloat16 [2304, 9216], P('blk', ('heads', 'section')), may hold values from -0.125 to 0.125
- down_weight: bfloat16 [9216, 2304], P(('heads', 'section'), 'blk'), may hold values from -0.0625 to 0.0625
- post_ffn_gain: float32 [2304], replicated, may hold values from 0.1 to 1.9
Outputs:
- scored_states: bfloat16 [4096, 2304], P(('groups', 'blk', 'heads', 'section')), parts along dimension 0
There are 2 independent parts, one for each index of `groups`. A program takes and returns all parts, laid end to end along the dimension named above; an argument that names none is the same for every part. Nothing has to cross between parts.
All inputs are finite; a program needn't handle non-finite values.
Results may differ from a plain program's by a relative error of at most 0.02.
Values may be sent and summed in bfloat16 or wider, within the bound.
A program may use at most 128 MiB of HBM per device.

v0:
```python
import jax
import jax.numpy as jnp
from jax import lax
from jax.sharding import PartitionSpec as P

HD = 256
GROUP = 2


softcap_limit = 50.0


def from_partner(block, axis, bit):
    count = lax.axis_size(axis)
    route = []
    for low in range(count):
        high = low | 1 << bit
        if high != low and high < count:
            route += [(low, high), (high, low)]
    return lax.ppermute(block, axis, route)


def rms_scale(values, gain):
    return values * lax.rsqrt(jnp.mean(values * values, axis=-1, keepdims=True) + 1e-06) * gain


def capped_scores(queries, keys):
    raw = lax.dot_general(
        queries, keys, (((1,), (1,)), ((), ())), preferred_element_type=jnp.float32
    ) * HD ** (-0.5)
    return softcap_limit * jnp.tanh(raw / softcap_limit)


def body(
    dec_states,
    cross_keys,
    cross_values,
    attn_gain,
    query_weight,
    out_weight,
    post_attn_gain,
    ffn_gain,
    gate_weight,
    up_weight,
    down_weight,
    post_ffn_gain,
):
    head_index = lax.axis_index("heads")
    kv_index = head_index // GROUP
    keys_local = lax.dynamic_index_in_dim(cross_keys, kv_index, 1, keepdims=False)
    values_local = lax.dynamic_index_in_dim(cross_values, kv_index, 1, keepdims=False)
    gate_full, up_full, down_full = (
        lax.all_gather(gate_weight, "blk", axis=0, tiled=True),
        lax.all_gather(up_weight, "blk", axis=0, tiled=True),
        lax.all_gather(down_weight, "blk", axis=1, tiled=True),
    )
    states = dec_states.astype(jnp.float32)
    normed = rms_scale(states, attn_gain).astype(jnp.bfloat16)
    queries = jnp.dot(normed, query_weight, preferred_element_type=jnp.float32).astype(jnp.bfloat16)
    rows_here = queries.shape[0]
    probs = jnp.exp(capped_scores(queries, lax.all_gather(keys_local, "blk", axis=0, tiled=True)))
    numer = jnp.dot(
        probs.astype(jnp.bfloat16),
        lax.all_gather(values_local, "blk", axis=0, tiled=True),
        preferred_element_type=jnp.float32,
    )
    numer, denom = (numer, jnp.sum(probs, axis=1))
    context = (numer / denom[:, None]).astype(jnp.bfloat16)
    head_term = jnp.dot(context, out_weight, preferred_element_type=jnp.float32)
    attended = lax.psum(head_term.astype(jnp.bfloat16), "heads").astype(jnp.float32)
    residual = (states + rms_scale(attended, post_attn_gain)).astype(jnp.bfloat16)
    ffn_input = rms_scale(residual.astype(jnp.float32), ffn_gain).astype(jnp.bfloat16)
    section_size = lax.axis_size("section")
    section_index = lax.axis_index("section")
    out_rows = rows_here // lax.axis_size("heads")
    block_index = head_index * section_size + section_index
    ffn_rows = lax.all_gather(ffn_input, "section", axis=0, tiled=True)
    partner_block = head_index * section_size + (1 - section_index)
    send_start = jnp.clip(
        partner_block * out_rows - section_index * rows_here, 0, rows_here - out_rows
    )
    outgoing = lax.dynamic_slice_in_dim(residual, send_start, out_rows, 0)
    incoming = from_partner(outgoing, "section", 0)
    own_start = jnp.clip(
        block_index * out_rows - section_index * rows_here, 0, rows_here - out_rows
    )
    local_rows = lax.dynamic_slice_in_dim(residual, own_start, out_rows, 0)
    holder = block_index * out_rows // rows_here
    residual_out = jnp.where(holder == section_index, local_rows, incoming)
    gate = jnp.dot(ffn_rows, gate_full, preferred_element_type=jnp.float32)
    up_part = jnp.dot(ffn_rows, up_full, preferred_element_type=jnp.float32)
    hidden = (jax.nn.gelu(gate, approximate=True) * up_part).astype(jnp.bfloat16)
    terms = jnp.dot(hidden, down_full, preferred_element_type=jnp.float32)
    ffn_out = lax.psum_scatter(
        terms.astype(jnp.bfloat16), ("heads", "section"), scatter_dimension=0, tiled=True
    ).astype(jnp.float32)
    return (residual_out.astype(jnp.float32) + rms_scale(ffn_out, post_ffn_gain)).astype(
        jnp.bfloat16
    )


def solution(mesh):
    in_specs = (
        P(("groups", "blk", "section"), None),
        P(("groups", "blk"), None, None),
        P(("groups", "blk"), None, None),
        P(),
        P(None, "heads"),
        P("heads", None),
        P(),
        P(),
        P("blk", ("heads", "section")),
        P("blk", ("heads", "section")),
        P(("heads", "section"), "blk"),
        P(),
    )
    out_specs = P(("groups", "blk", "heads", "section"), None)
    return jax.shard_map(body, mesh=mesh, in_specs=in_specs, out_specs=out_specs, check_vma=False)
```

profile of v0, /device:TPU:0, one launch (start us, length us, event | category | flops | bytes accessed | tf_op | source)
XLA Modules:
  0.0 726.4 jit_solution(15588221195975664672)
XLA Ops:
  6.5 16.0 %all-gather = bf16[512,1,256]{2,0,1:T(8,128)(2,1)S(1)} all-gather(bf16[128,1,256]{2,0,1:T(8,128)(2,1)} %param.13), channel_id=2, replica_groups=mesh['groups'=2,'blk'=4,'heads'=2,'section'=2] {'blk'}, dimensions={0}, use_global_device_ids=true | all-gather | bytes 327680 | tf_op jit(solution)/shard_map/all_gather | solution.py:61
  22.5 1.6 fusion.13
  24.1 14.8 %all-gather.1 = bf16[512,1,256]{2,0,1:T(8,128)(2,1)S(1)} all-gather(bf16[128,1,256]{2,0,1:T(8,128)(2,1)} %param.14), channel_id=3, replica_groups=mesh['groups'=2,'blk'=4,'heads'=2,'section'=2] {'blk'}, dimensions={0}, use_global_device_ids=true | all-gather | bytes 327680 | tf_op jit(solution)/shard_map/all_gather | solution.py:64
  38.9 2.6 fusion.45
  41.4 1.7 convolution_convert_fusion.1
  43.2 0.0 all-gather.7.cloned.1.call-start
  43.3 43.9 %all-reduce.2.cloned.1.call-done = bf16[256,2304]{1,0:T(8,128)(2,1)} async-done(((bf16[256,2304]{1,0:T(8,128)(2,1)}), bf16[256,2304]{1,0:T(8,128)(2,1)}) %all-reduce.2.cloned.1.call-update) | async-done | bytes 1179664 | tf_op jit(solution)/shard_map/psum | solution.py:70
  87.1 1.6 fusion.8
  88.7 2.0 fusion.10
  90.7 1.4 fusion.12
  92.2 0.7 all-gather.9.cloned.1.call-update
  92.9 0.5 all-gather.11.cloned.1.call-update
  93.5 0.5 all-gather.13.cloned.1.call-update
  94.1 9.2 %all-gather.7.cloned.1.call-done = bf16[512,2304]{1,0:T(8,128)(2,1)} async-done(((bf16[256,2304]{1,0:T(8,128)(2,1)}), bf16[512,2304]{1,0:T(8,128)(2,1)}) %all-gather.7.cloned.1.call-update) | async-done | bytes 2359312 | tf_op jit(solution)/shard_map/all_gather | solution.py:77
  103.3 188.9 %all-gather.9.cloned.1.call-done = bf16[2304,2304]{1,0:T(8,128)(2,1)} async-done(((bf16[576,2304]{1,0:T(8,128)(2,1)}), bf16[2304,2304]{1,0:T(8,128)(2,1)}) %all-gather.9.cloned.1.call-update) | async-done | bytes 10616848 | tf_op jit(solution)/shard_map/all_gather | solution.py:53
  292.2 11.6 %fusion.48 = f32[512,2304]{1,0:T(8,128)} fusion(bf16[512,2304]{1,0:T(8,128)(2,1)} %all-gather.7.cloned.1.call-done, bf16[2304,2304]{1,0:T(8,128)(2,1)} %all-gather.9.cloned.1.call-done), kind=kOutput, calls=%fused_computation.58 | convolution fusion | flops 5435817984 | bytes 17694720 | tf_op jit(solution)/shard_map/dot_general | solution.py:90
  303.8 174.2 %all-gather.11.cloned.1.call-done = bf16[2304,2304]{1,0:T(8,128)(2,1)} async-done(((bf16[576,2304]{1,0:T(8,128)(2,1)}), bf16[2304,2304]{1,0:T(8,128)(2,1)}) %all-gather.11.cloned.1.call-update) | async-done | bytes 10616848 | tf_op jit(solution)/shard_map/all_gather | solution.py:54
  478.0 185.8 %all-gather.13.cloned.1.call-done = bf16[2304,2304]{0,1:T(8,128)(2,1)} async-done(((bf16[2304,576]{0,1:T(8,128)(2,1)}), bf16[2304,2304]{0,1:T(8,128)(2,1)}) %all-gather.13.cloned.1.call-update) | async-done | bytes 10616848 | tf_op jit(solution)/shard_map/all_gather | solution.py:55
  663.8 20.7 %convolution_convert_fusion = bf16[512,2304]{1,0:T(8,128)(2,1)} fusion(bf16[2304,2304]{0,1:T(8,128)(2,1)} %all-gather.13.cloned.1.call-done, bf16[512,2304]{1,0:T(8,128)(2,1)} %all-gather.7.cloned.1.call-done, bf16[2304,2304]{1,0:T(8,128)(2,1)} %all-gather.11.cloned.1.call-done, f32[512,2304]{1,0:T(8,128)} %fusion.48), kind=kOutput, calls=%fused_computation.10 | convolution fusion | flops 10884612096 | bytes 30670848 | tf_op jit(solution)/shard_map/dot_general | solution.py:93
  684.5 0.1 constant_dynamic-slice_fusion
  684.7 0.1 collective-permute-start
  684.8 31.1 %reduce-scatter.2.cloned.1.call-done = bf16[128,2304]{1,0:T(8,128)(2,1)} async-done(((bf16[512,2304]{1,0:T(8,128)(2,1)}), bf16[128,2304]{1,0:T(8,128)(2,1)}) %reduce-scatter.2.cloned.1.call-update) | async-done | bytes 589840 | tf_op jit(solution)/shard_map/reduce_scatter | solution.py:94
  715.9 1.3 fusion.20
  717.2 2.3 fusion.23
  (21 shorter events, 0.3 us)
Async XLA Ops:
  6.5 34.9 %copy-start = (bf16[256,2304]{1,0:T(8,128)(2,1)S(1)}, bf16[256,2304]{1,0:T(8,128)(2,1)}, u32[]{:S(2)}) copy-start(bf16[256,2304]{1,0:T(8,128)(2,1)} %param.17) | copy-start | bytes 3538948
  6.5 80.6 %all-reduce.2.cloned.1.call-start = ((), (), s32[]{:S(2)}) async-start(), calls=%async_computation.1 | async-start | bytes 2359296 | tf_op jit(solution)/shard_map/psum | solution.py:70
  41.4 47.3 %copy-start.1 = (bf16[256,2304]{1,0:T(8,128)(2,1)S(1)}, bf16[256,2304]{1,0:T(8,128)(2,1)}, u32[]{:S(2)}) copy-start(bf16[256,2304]{1,0:T(8,128)(2,1)} %param.12) | copy-start | bytes 3538948
  43.2 47.5 %copy-start.2 = (f32[2304]{0:T(1024)S(1)}, f32[2304]{0:T(1024)}, u32[]{:S(2)}) copy-start(f32[2304]{0:T(1024)} %param.19) | copy-start | bytes 27652
  43.2 60.1 %all-gather.7.cloned.1.call-start = ((), (), s32[]{:S(2)}) async-start(), calls=%async_computation.2 | async-start | bytes 3538944 | tf_op jit(solution)/shard_map/all_gather | solution.py:77
  92.1 200.0 %all-gather.9.cloned.1.call-start = ((), (), s32[]{:S(2)}) async-start(), calls=%async_computation.3 | async-start | bytes 13271040 | tf_op jit(solution)/shard_map/all_gather | solution.py:53
  92.9 385.1 %all-gather.11.cloned.1.call-start = ((), (), s32[]{:S(2)}) async-start(), calls=%async_computation.4 | async-start | bytes 13271040 | tf_op jit(solution)/shard_map/all_gather | solution.py:54
  93.5 570.3 %all-gather.13.cloned.1.call-start = ((), (), s32[]{:S(2)}) async-start(), calls=%async_computation.5 | async-start | bytes 13271040 | tf_op jit(solution)/shard_map/all_gather | solution.py:55
  94.1 621.9 %reduce-scatter.2.cloned.1.call-start = ((), (), s32[]{:S(2)}) async-start(), calls=%async_computation.6 | async-start | bytes 2949120 | tf_op jit(solution)/shard_map/reduce_scatter | solution.py:94
  684.5 32.7 %copy-start.3 = (f32[2304]{0:T(1024)S(1)}, f32[2304]{0:T(1024)}, u32[]{:S(2)}) copy-start(f32[2304]{0:T(1024)} %param.23) | copy-start | bytes 27652
  684.7 32.5 %collective-permute-start = (bf16[128,2304]{1,0:T(8,128)(2,1)S(1)}, bf16[128,2304]{1,0:T(8,128)(2,1)S(1)}, u32[]{:S(2)}, u32[]{:S(2)}) collective-permute-start(bf16[128,2304]{1,0:T(8,128)(2,1)S(1)} %constant_dynamic-slice_fusion), channel_id=1, source_target_pairs={{0,1},{1,0},{2,3},{3,2},{4,5},{5,4},{6,7},{7,6},{8,9},{9,8},{10,11... | collective-permute-start | bytes 1769480 | tf_op jit(solution)/shard_map/ppermute | solution.py:20
Sparse Core Ops, SparseCore 0:
  43.3 43.7 all-reduce.1
  92.3 10.9 all-gather.6
  104.9 187.2 all-gather.8
  293.7 184.2 all-gather.10
  479.5 184.2 all-gather.12
  684.7 31.2 reduce-scatter.1
where the time goes:
time: 727 us; the launch traced here: 726 us
  waiting for transfers between devices  635 us (87%)
  matrix products  36.7 us (5%)
  blocking collectives  30.7 us (4%)
  between operations  13.6 us (2%)
  other arithmetic  10.1 us (1%)
    all_gather x1, waiting for transfers between devices, body(): lax.all_gather(gate_weight, 'blk', axis=0, tiled=True)  189 us
    all_gather x1, waiting for transfers between devices, body(): lax.all_gather(down_weight, 'blk', axis=1, tiled=True)  186 us
    all_gather x1, waiting for transfers between devices, body(): lax.all_gather(up_weight, 'blk', axis=0, tiled=True)  174 us
    psum x1, waiting for transfers between devices, body(): lax.psum(head_term.astype(jnp.bfloat16), 'heads').astype(jnp.float32)  43.9 us
    reduce_scatter x1, waiting for transfers between devices, body(): lax.psum_scatter(terms.astype(jnp.bfloat16), ('heads', 'section'), scatte...  31.1 us
    dot_general x1, matrix products, body(): terms = jnp.dot(hidden, down_full, preferred_element_type=jnp.float32)  20.7 us
    all_gather x1, blocking collectives, body(): lax.all_gather(keys_local, 'blk', axis=0, tiled=True)  16 us
    all_gather x1, blocking collectives, body(): lax.all_gather(values_local, 'blk', axis=0, tiled=True)  14.8 us
  transfers between devices with their start and end apart: 7, of which 6 were waited for; matrix products, arithmetic and copies ran while one was open for 2% of the time, Pallas kernels for 0%

commit v1 on v0

--- a/solution.py
+++ b/solution.py
@@ -31,7 +31,35 @@
     return softcap_limit * jnp.tanh(raw / softcap_limit)
 
 
-def body(
+def reshard_over_blk(weight, split_axis, concat_axis):
+    count = lax.axis_size("blk")
+    groups = lax.axis_size("groups")
+    me = lax.axis_index("blk")
+    my_group = lax.axis_index("groups")
+    piece = weight.shape[split_axis] // count
+    depth = weight.shape[concat_axis]
+    shape = [piece, piece]
+    shape[concat_axis] = depth * count
+    sizes = [piece, piece]
+    sizes[concat_axis] = depth
+    half = sizes[0] // groups
+    whole = jnp.zeros(shape, weight.dtype)
+    own = lax.dynamic_slice_in_dim(weight, me * piece, piece, split_axis)
+    whole = lax.dynamic_update_slice_in_dim(whole, own, me * depth, concat_axis)
+    for step in range(1, count):
+        peer = me ^ step
+        packet = lax.dynamic_slice_in_dim(weight, peer * piece, piece, split_axis)
+        packet = lax.dynamic_slice_in_dim(packet, my_group * half, half, 0)
+        first = lax.ppermute(packet, "blk", [(i, i ^ step) for i in range(count)])
+        second = lax.ppermute(first, "groups", [(0, 1), (1, 0)])
+        for part, group in ((first, my_group), (second, 1 - my_group)):
+            at = [group * half, 0]
+            at[concat_axis] += peer * depth
+            whole = lax.dynamic_update_slice(whole, part, at)
+    return whole
+
+
+def weights_body(
     dec_states,
     cross_keys,
     cross_values,
@@ -99,6 +127,73 @@
     )
 
 
+def rows_body(
+    dec_states,
+    cross_keys,
+    cross_values,
+    attn_gain,
+    query_weight,
+    out_weight,
+    post_attn_gain,
+    ffn_gain,
+    gate_weight,
+    up_weight,
+    down_weight,
+    post_ffn_gain,
+):
+    head_index = lax.axis_index("heads")
+    kv_index = head_index // GROUP
+    keys_local = lax.dynamic_index_in_dim(cross_keys, kv_index, 1, keepdims=False)
+    values_local = lax.dynamic_index_in_dim(cross_values, kv_index, 1, keepdims=False)
+    kv_all = lax.all_gather(jnp.stack([keys_local, values_local]), "blk", axis=1, tiled=True)
+    gate_mine = reshard_over_blk(gate_weight, 1, 0)
+    up_mine = reshard_over_blk(up_weight, 1, 0)
+    down_mine = reshard_over_blk(down_weight, 0, 1)
+    states = dec_states.astype(jnp.float32)
+    normed = rms_scale(states, attn_gain).astype(jnp.bfloat16)
+    queries = jnp.dot(normed, query_weight, preferred_element_type=jnp.float32).astype(jnp.bfloat16)
+    probs = jnp.exp(capped_scores(queries, kv_all[0]))
+    numer = jnp.dot(probs.astype(jnp.bfloat16), kv_all[1], preferred_element_type=jnp.float32)
+    denom = jnp.sum(probs, axis=1)
+    context = (numer / denom[:, None]).astype(jnp.bfloat16)
+    head_term = jnp.dot(context, out_weight, preferred_element_type=jnp.float32).astype(jnp.bfloat16)
+    heads = lax.axis_size("heads")
+    section_size = lax.axis_size("section")
+    section_index = lax.axis_index("section")
+    attended = lax.psum_scatter(head_term, "heads", scatter_dimension=0, tiled=True).astype(jnp.float32)
+    out_rows = attended.shape[0]
+    kept = lax.dynamic_slice_in_dim(dec_states, head_index * out_rows, out_rows, 0).astype(jnp.float32)
+    residual = (kept + rms_scale(attended, post_attn_gain)).astype(jnp.bfloat16)
+    ffn_input = rms_scale(residual.astype(jnp.float32), ffn_gain).astype(jnp.bfloat16)
+    route = [
+        (h * section_size + s, s * heads + h) for h in range(heads) for s in range(section_size)
+    ]
+    residual_out = lax.ppermute(residual, ("heads", "section"), route)
+    ffn_rows = lax.all_gather(ffn_input, ("blk", "section", "heads"), axis=0, tiled=True)
+    gate = jnp.dot(ffn_rows, gate_mine, preferred_element_type=jnp.float32)
+    up_part = jnp.dot(ffn_rows, up_mine, preferred_element_type=jnp.float32)
+    hidden = (jax.nn.gelu(gate, approximate=True) * up_part).astype(jnp.bfloat16)
+    terms = jnp.dot(hidden, down_mine, preferred_element_type=jnp.float32).astype(jnp.bfloat16)
+    ffn_out = lax.psum_scatter(
+        terms, ("blk", "heads", "section"), scatter_dimension=0, tiled=True
+    ).astype(jnp.float32)
+    return (residual_out.astype(jnp.float32) + rms_scale(ffn_out, post_ffn_gain)).astype(
+        jnp.bfloat16
+    )
+
+
+def rows_travel(mesh, dec_states, gate_weight):
+    blk, heads, section, groups = (mesh.shape[a] for a in ("blk", "heads", "section", "groups"))
+    width = dec_states.shape[1]
+    rows = dec_states.shape[0] // groups
+    units = gate_weight.shape[1] // (heads * section)
+    gathered = 3 * width * units
+    moved = 3 * width * units // blk + 2 * rows * width
+    power = blk & (blk - 1) == 0
+    fits = units % (blk * groups) == 0 and width % (blk * groups) == 0
+    return groups == 2 and power and fits and moved < gathered
+
+
 def solution(mesh):
     in_specs = (
         P(("groups", "blk", "section"), None),
@@ -115,4 +210,11 @@
         P(),
     )
     out_specs = P(("groups", "blk", "heads", "section"), None)
-    return jax.shard_map(body, mesh=mesh, in_specs=in_specs, out_specs=out_specs, check_vma=False)
+
+    def layer(*args):
+        plan = rows_body if rows_travel(mesh, args[0], args[8]) else weights_body
+        return jax.shard_map(
+            plan, mesh=mesh, in_specs=in_specs, out_specs=out_specs, check_vma=False
+        )(*args)
+
+    return layer

time: 727 us -> 404 us (0.56)
  waiting for transfers between devices: 635 us -> 202 us
  local copies, waits for them, and re-layouts: 0.17 us -> 69.4 us
  starting transfers between devices: 0.32 us -> 49.8 us
  blocking collectives: 30.7 us -> 17.4 us
    all_gather x4 -> x1, waiting for transfers between devices: 558 us -> 0.01 us  [rows_body(): lax.all_gather(ffn_input, ('blk', 'section', 'heads'), axis=0, tiled=True)]
    reduce_scatter x1 -> x2, waiting for transfers between devices: 31.1 us -> 134 us  [the longest x1 110 us: rows_body(): lax.psum_scatter(terms, ('blk', 'heads', 'section'), scatter_dimension=0,...]
    ppermute x1 -> x19, waiting for transfers between devices: 0.01 us -> 68 us  [the longest x9 60.9 us: reshard_over_blk(): first = lax.ppermute(packet, 'blk', [(i, i ^ step) for i in range(count)])]
    dynamic_update_slice x0 -> x21, local copies, waits for them, and re-layouts: none -> 56.7 us  [the longest x18 50.5 us: reshard_over_blk(): whole = lax.dynamic_update_slice(whole, part, at)]
    ppermute x1 -> x19, starting transfers between devices: 0.12 us -> 49.5 us  [the longest x9 38.3 us: reshard_over_blk(): first = lax.ppermute(packet, 'blk', [(i, i ^ step) for i in range(count)])]
    psum x1 -> x0, waiting for transfers between devices: 43.9 us -> none  [body(): lax.psum(head_term.astype(jnp.bfloat16), 'heads').astype(jnp.float32)]
    all_gather x2 -> x1, blocking collectives: 30.7 us -> 17.4 us  [rows_body(): lax.all_gather(jnp.stack([keys_local, values_local]), 'blk', axis=1, tile...]
    dynamic_slice x1 -> x3, local copies, waits for them, and re-layouts: 0.15 us -> 8.69 us  [reshard_over_blk(): packet = lax.dynamic_slice_in_dim(packet, my_group * half, half, 0)]
  transfers between devices with their start and end apart: 7 -> 22, of which waited for: 6 -> 7; matrix products, arithmetic and copies ran while one was open for 2% -> 18% of each run, Pallas kernels for 0% -> 0%
where the time goes in v1:
time: 404 us; the launch traced here: 402 us
  waiting for transfers between devices  202 us (50%)
  local copies, waits for them, and re-layouts  69.4 us (17%)
  starting transfers between devices  49.8 us (12%)
  matrix products  40.3 us (10%)
  blocking collectives  17.4 us (4%)
  between operations  13.3 us (3%)
  other arithmetic  9.82 us (2%)
    reduce_scatter x1, waiting for transfers between devices, rows_body(): lax.psum_scatter(terms, ('blk', 'heads', 'section'), scatter_dimension=0,...  110 us
    ppermute x9, waiting for transfers between devices, reshard_over_blk(): first = lax.ppermute(packet, 'blk', [(i, i ^ step) for i in range(count)])  60.9 us
    dynamic_update_slice x18, local copies, waits for them, and re-layouts, reshard_over_blk(): whole = lax.dynamic_update_slice(whole, part, at)  50.5 us
    ppermute x9, starting transfers between devices, reshard_over_blk(): first = lax.ppermute(packet, 'blk', [(i, i ^ step) for i in range(count)])  38.3 us
    dot_general x1, matrix products, rows_body(): jnp.dot(hidden, down_mine, preferred_element_type=jnp.float32)  25.3 us
    reduce_scatter x1, waiting for transfers between devices, rows_body(): lax.psum_scatter(head_term, 'heads', scatter_dimension=0, tiled=True)  23.6 us
    all_gather x1, blocking collectives, rows_body(): lax.all_gather(jnp.stack([keys_local, values_local]), 'blk', axis=1, tile...  17.4 us
    dot_general x1, matrix products, rows_body(): gate = jnp.dot(ffn_rows, gate_mine, preferred_element_type=jnp.float32)  10.7 us
  transfers between devices with their start and end apart: 22, of which 7 were waited for; matrix products, arithmetic and copies ran while one was open for 18% of the time, Pallas kernels for 0%

profile of v1, /device:TPU:0, one launch (start us, length us, event | category | flops | bytes accessed | tf_op | source)
XLA Modules:
  0.0 401.6 jit_solution(11174122113614041856)
XLA Ops:
  9.1 17.4 %all_gather.6 = bf16[2,512,256]{2,1,0:T(8,128)(2,1)S(1)} all-gather(bf16[2,128,256]{2,1,0:T(8,128)(2,1)S(1)} %pad_maximum_fusion), channel_id=1, replica_groups=mesh['groups'=2,'blk'=4,'heads'=2,'section'=2] {'blk'}, dimensions={1}, use_global_device_ids=true | all-gather | bytes 655360 | tf_op jit(solution)/shard_map/all_gather | solution.py:148
  26.5 2.5 fusion.51
  30.9 23.6 %reduce-scatter.3.cloned.1.call-done = bf16[128,2304]{1,0:T(8,128)(2,1)} async-done(((bf16[256,2304]{1,0:T(8,128)(2,1)}), bf16[128,2304]{1,0:T(8,128)(2,1)}) %reduce-scatter.3.cloned.1.call-update) | async-done | bytes 589840 | tf_op jit(solution)/shard_map/reduce_scatter | solution.py:163
  58.7 2.8 fusion.49
  61.5 3.3 collective-permute-start.5
  64.9 2.9 constant_dynamic-slice_fusion.1
  72.2 3.0 fusion.50
  75.1 4.9 %collective-permute-done.5 = bf16[288,576]{1,0:T(8,128)(2,1)} collective-permute-done((bf16[288,576]{1,0:T(8,128)(2,1)S(1)}, bf16[288,576]{1,0:T(8,128)(2,1)}, u32[]{:S(2)}, u32[]{:S(2)}) %collective-permute-start.5) | collective-permute-done | bytes 331808 | tf_op jit(solution)/shard_map/ppermute | solution.py:53
  80.1 27.5 %collective-permute-start.7 = (bf16[288,576]{1,0:T(8,128)(2,1)}, bf16[288,576]{1,0:T(8,128)(2,1)}, u32[]{:S(2)}, u32[]{:S(2)}) collective-permute-start(bf16[288,576]{1,0:T(8,128)(2,1)} %get-tuple-element.11), channel_id=1, source_target_pairs={{0,4},{4,0},{8,12},{12,8},{1,5},{5,1},{9,13},{13,9},{2,6},{6,2},{1... | collective-permute-start | bytes 995336 | tf_op jit(solution)/shard_map/ppermute | solution.py:53
  109.1 2.7 collective-permute-done.13
  115.0 43.0 %collective-permute-done.15 = bf16[288,576]{0,1:T(8,128)(2,1)S(1)} collective-permute-done((bf16[288,576]{0,1:T(8,128)(2,1)}, bf16[288,576]{0,1:T(8,128)(2,1)S(1)}, u32[]{:S(2)}, u32[]{:S(2)}) %collective-permute-start.15) | collective-permute-done | bytes 331808 | tf_op jit(solution)/shard_map/ppermute | solution.py:53
  161.4 2.4 dynamic-slice_dynamic-update-slice_fusion
  169.2 2.4 dynamic-slice_dynamic-update-slice_fusion.1
  171.6 5.6 %dynamic_update_slice.78 = bf16[576,2304]{0,1:T(8,128)(2,1)} dynamic-update-slice(bf16[576,2304]{0,1:T(8,128)(2,1)} %dynamic-slice_dynamic-update-slice_fusion, bf16[288,576]{0,1:T(8,128)(2,1)S(1)} %collective-permute-done.13, s32[]{:T(128)S(6)} %select_n.42, s32[]{:T(128)S(6)} %select_n.44) | dynamic-update-slice | bytes 663556 | tf_op jit(solution)/shard_map/dynamic_update_slice | solution.py:58
  182.3 6.0 %dynamic_update_slice.79 = bf16[576,2304]{0,1:T(8,128)(2,1)} dynamic-update-slice(bf16[576,2304]{0,1:T(8,128)(2,1)} %dynamic_update_slice.78, bf16[288,576]{0,1:T(8,128)(2,1)} %collective-permute-done.14, s32[]{:T(128)S(6)} %select_n.105, s32[]{:T(128)S(6)} %select_n.44) | dynamic-update-slice | bytes 663556 | tf_op jit(solution)/shard_map/dynamic_update_slice | solution.py:58
  188.3 5.7 %dynamic_update_slice.80 = bf16[576,2304]{0,1:T(8,128)(2,1)} dynamic-update-slice(bf16[576,2304]{0,1:T(8,128)(2,1)} %dynamic_update_slice.79, bf16[288,576]{0,1:T(8,128)(2,1)S(1)} %collective-permute-done.15, s32[]{:T(128)S(6)} %select_n.42, s32[]{:T(128)S(6)} %select_n.48) | dynamic-update-slice | bytes 663556 | tf_op jit(solution)/shard_map/dynamic_update_slice | solution.py:58
  193.9 5.9 %dynamic_update_slice.81 = bf16[576,2304]{0,1:T(8,128)(2,1)} dynamic-update-slice(bf16[576,2304]{0,1:T(8,128)(2,1)} %dynamic_update_slice.80, bf16[288,576]{0,1:T(8,128)(2,1)} %collective-permute-done.16, s32[]{:T(128)S(6)} %select_n.105, s32[]{:T(128)S(6)} %select_n.48) | dynamic-update-slice | bytes 663556 | tf_op jit(solution)/shard_map/dynamic_update_slice | solution.py:58
  199.9 5.5 %dynamic_update_slice.82 = bf16[576,2304]{0,1:T(8,128)(2,1)} dynamic-update-slice(bf16[576,2304]{0,1:T(8,128)(2,1)} %dynamic_update_slice.81, bf16[288,576]{0,1:T(8,128)(2,1)S(1)} %collective-permute-done.17, s32[]{:T(128)S(6)} %select_n.42, s32[]{:T(128)S(6)} %select_n.52) | dynamic-update-slice | bytes 663556 | tf_op jit(solution)/shard_map/dynamic_update_slice | solution.py:58
  205.3 5.5 %dynamic_update_slice.83 = bf16[576,2304]{0,1:T(8,128)(2,1)} dynamic-update-slice(bf16[576,2304]{0,1:T(8,128)(2,1)} %dynamic_update_slice.82, bf16[288,576]{0,1:T(8,128)(2,1)S(1)} %collective-permute-done.18, s32[]{:T(128)S(6)} %select_n.105, s32[]{:T(128)S(6)} %select_n.52) | dynamic-update-slice | bytes 663556 | tf_op jit(solution)/shard_map/dynamic_update_slice | solution.py:58
  212.9 10.2 %collective-permute-done.9 = bf16[288,576]{1,0:T(8,128)(2,1)} collective-permute-done((bf16[288,576]{1,0:T(8,128)(2,1)}, bf16[288,576]{1,0:T(8,128)(2,1)}, u32[]{:S(2)}, u32[]{:S(2)}) %collective-permute-start.9) | collective-permute-done | bytes 331808 | tf_op jit(solution)/shard_map/ppermute | solution.py:53
  233.7 7.1 %collective-permute-done.10 = bf16[288,576]{1,0:T(8,128)(2,1)S(1)} collective-permute-done((bf16[288,576]{1,0:T(8,128)(2,1)}, bf16[288,576]{1,0:T(8,128)(2,1)S(1)}, u32[]{:S(2)}, u32[]{:S(2)}) %collective-permute-start.10) | collective-permute-done | bytes 331808 | tf_op jit(solution)/shard_map/ppermute | solution.py:54
  244.9 10.7 %fusion.56 = f32[2048,576]{0,1:T(8,128)} fusion(bf16[2048,2304]{1,0:T(8,128)(2,1)} %all-gather.2.cloned.1.call-done, bf16[2304,576]{1,0:T(8,128)(2,1)} %constant_dynamic-update-slice_fusion.6), kind=kOutput, calls=%fused_computation.83 | convolution fusion | flops 5435817984 | bytes 16809984 | tf_op jit(solution)/shard_map/dot_general | solution.py:173
  255.6 25.3 %convolution_convert_fusion = bf16[2048,2304]{1,0:T(8,128)(2,1)} fusion(bf16[576,2304]{0,1:T(8,128)(2,1)} %dynamic_update_slice.83, f32[2048,576]{0,1:T(8,128)} %fusion.56, bf16[2048,2304]{1,0:T(8,128)(2,1)} %all-gather.2.cloned.1.call-done, bf16[2304,576]{1,0:T(8,128)(2,1)} %constant_dynamic-update-slice_fusion), kind=kOutput, calls=%fused_computation | convolution fusion | flops 10888151040 | bytes 28901376 | tf_op jit(solution)/shard_map/dot_general | solution.py:176
  281.6 110.0 %reduce-scatter.5.cloned.1.call-done = bf16[128,2304]{1,0:T(8,128)(2,1)} async-done(((bf16[2048,2304]{1,0:T(8,128)(2,1)}), bf16[128,2304]{1,0:T(8,128)(2,1)}) %reduce-scatter.5.cloned.1.call-update) | async-done | bytes 589840 | tf_op jit(solution)/shard_map/reduce_scatter | solution.py:177
  (78 shorter events, 52.3 us)
Async XLA Ops:
  6.5 48.0 %reduce-scatter.3.cloned.1.call-start = ((), (), s32[]{:S(2)}) async-start(), calls=%async_computation.2 | async-start | bytes 1769472 | tf_op jit(solution)/shard_map/reduce_scatter | solution.py:163
  30.9 214.0 %all-gather.2.cloned.1.call-start = ((), (), s32[]{:S(2)}) async-start(), calls=%async_computation.3 | async-start | bytes 10027008 | tf_op jit(solution)/shard_map/all_gather | solution.py:172
  58.4 333.2 %reduce-scatter.5.cloned.1.call-start = ((), (), s32[]{:S(2)}) async-start(), calls=%async_computation.4 | async-start | bytes 10027008 | tf_op jit(solution)/shard_map/reduce_scatter | solution.py:177
  61.5 18.6 %collective-permute-start.5 = (bf16[288,576]{1,0:T(8,128)(2,1)S(1)}, bf16[288,576]{1,0:T(8,128)(2,1)}, u32[]{:S(2)}, u32[]{:S(2)}) collective-permute-start(bf16[288,576]{1,0:T(8,128)(2,1)S(1)} %get-tuple-element.7), channel_id=1, source_target_pairs={{0,12},{4,8},{8,4},{12,0},{1,13},{5,9},{9,5},{13,1},{2,14},{6,10},... | collective-permute-start | bytes 995336 | tf_op jit(solution)/shard_map/ppermute | solution.py:53
  67.8 39.8 %collective-permute-start.17 = (bf16[288,576]{0,1:T(8,128)(2,1)S(1)}, bf16[288,576]{0,1:T(8,128)(2,1)S(1)}, u32[]{:S(2)}, u32[]{:S(2)}) collective-permute-start(bf16[288,576]{0,1:T(8,128)(2,1)S(1)} %get-tuple-element.13), channel_id=1, source_target_pairs={{0,12},{4,8},{8,4},{12,0},{1,13},{5,9},{9,5},{13,1},{2,14},{6,10},... | collective-permute-start | bytes 995336 | tf_op jit(solution)/shard_map/ppermute | solution.py:53
  68.1 43.7 %collective-permute-start.13 = (bf16[288,576]{0,1:T(8,128)(2,1)S(1)}, bf16[288,576]{0,1:T(8,128)(2,1)S(1)}, u32[]{:S(2)}, u32[]{:S(2)}) collective-permute-start(bf16[288,576]{0,1:T(8,128)(2,1)S(1)} %get-tuple-element.14), channel_id=1, source_target_pairs={{0,4},{4,0},{8,12},{12,8},{1,5},{5,1},{9,13},{13,9},{2,6},{6,2},{1... | collective-permute-start | bytes 995336 | tf_op jit(solution)/shard_map/ppermute | solution.py:53
  68.1 95.6 %collective-permute-start.1 = (bf16[288,576]{1,0:T(8,128)(2,1)}, bf16[288,576]{1,0:T(8,128)(2,1)}, u32[]{:S(2)}, u32[]{:S(2)}) collective-permute-start(bf16[288,576]{1,0:T(8,128)(2,1)} %get-tuple-element.8), channel_id=1, source_target_pairs={{0,4},{4,0},{8,12},{12,8},{1,5},{5,1},{9,13},{13,9},{2,6},{6,2},{1... | collective-permute-start | bytes 995336 | tf_op jit(solution)/shard_map/ppermute | solution.py:53
  70.1 87.9 %collective-permute-start.15 = (bf16[288,576]{0,1:T(8,128)(2,1)}, bf16[288,576]{0,1:T(8,128)(2,1)S(1)}, u32[]{:S(2)}, u32[]{:S(2)}) collective-permute-start(bf16[288,576]{0,1:T(8,128)(2,1)} %get-tuple-element.15), channel_id=1, source_target_pairs={{0,8},{4,12},{8,0},{12,4},{1,9},{5,13},{9,1},{13,5},{2,10},{6,14},... | collective-permute-start | bytes 995336 | tf_op jit(solution)/shard_map/ppermute | solution.py:53
  80.1 83.7 %collective-permute-start.7 = (bf16[288,576]{1,0:T(8,128)(2,1)}, bf16[288,576]{1,0:T(8,128)(2,1)}, u32[]{:S(2)}, u32[]{:S(2)}) collective-permute-start(bf16[288,576]{1,0:T(8,128)(2,1)} %get-tuple-element.11), channel_id=1, source_target_pairs={{0,4},{4,0},{8,12},{12,8},{1,5},{5,1},{9,13},{13,9},{2,6},{6,2},{1... | collective-permute-start | bytes 995336 | tf_op jit(solution)/shard_map/ppermute | solution.py:53
  107.6 57.0 %collective-permute-start.18 = (bf16[288,576]{0,1:T(8,128)(2,1)S(1)}, bf16[288,576]{0,1:T(8,128)(2,1)S(1)}, u32[]{:S(2)}, u32[]{:S(2)}) collective-permute-start(bf16[288,576]{0,1:T(8,128)(2,1)S(1)} %collective-permute-done.17), channel_id=1, source_target_pairs={{0,16},{16,0},{1,17},{17,1},{2,18},{18,2},{3,19},{19,3},{4,20},{20... | collective-permute-start | bytes 995336 | tf_op jit(solution)/shard_map/ppermute | solution.py:54
  111.8 55.0 %collective-permute-start.14 = (bf16[288,576]{0,1:T(8,128)(2,1)S(1)}, bf16[288,576]{0,1:T(8,128)(2,1)}, u32[]{:S(2)}, u32[]{:S(2)}) collective-permute-start(bf16[288,576]{0,1:T(8,128)(2,1)S(1)} %collective-permute-done.13), channel_id=1, source_target_pairs={{0,16},{16,0},{1,17},{17,1},{2,18},{18,2},{3,19},{19,3},{4,20},{20... | collective-permute-start | bytes 995336 | tf_op jit(solution)/shard_map/ppermute | solution.py:54
  115.0 54.2 %copy-start.1 = (bf16[2304,576]{1,0:T(8,128)(2,1)}, bf16[2304,576]{1,0:T(8,128)(2,1)S(1)}, u32[]{:S(2)}) copy-start(bf16[2304,576]{1,0:T(8,128)(2,1)S(1)} %dynamic-slice_dynamic-update-slice_fusion.2) | copy-start | bytes 7962628
  158.1 20.9 %collective-permute-start.16 = (bf16[288,576]{0,1:T(8,128)(2,1)S(1)}, bf16[288,576]{0,1:T(8,128)(2,1)}, u32[]{:S(2)}, u32[]{:S(2)}) collective-permute-start(bf16[288,576]{0,1:T(8,128)(2,1)S(1)} %collective-permute-done.15), channel_id=1, source_target_pairs={{0,16},{16,0},{1,17},{17,1},{2,18},{18,2},{3,19},{19,3},{4,20},{20... | collective-permute-start | bytes 995336 | tf_op jit(solution)/shard_map/ppermute | solution.py:54
  163.8 47.1 %collective-permute-start.3 = (bf16[288,576]{1,0:T(8,128)(2,1)}, bf16[288,576]{1,0:T(8,128)(2,1)}, u32[]{:S(2)}, u32[]{:S(2)}) collective-permute-start(bf16[288,576]{1,0:T(8,128)(2,1)} %get-tuple-element.9), channel_id=1, source_target_pairs={{0,8},{4,12},{8,0},{12,4},{1,9},{5,13},{9,1},{13,5},{2,10},{6,14},... | collective-permute-start | bytes 995336 | tf_op jit(solution)/shard_map/ppermute | solution.py:53
  163.8 47.5 %collective-permute-start.11 = (bf16[288,576]{1,0:T(8,128)(2,1)}, bf16[288,576]{1,0:T(8,128)(2,1)}, u32[]{:S(2)}, u32[]{:S(2)}) collective-permute-start(bf16[288,576]{1,0:T(8,128)(2,1)} %get-tuple-element.10), channel_id=1, source_target_pairs={{0,12},{4,8},{8,4},{12,0},{1,13},{5,9},{9,5},{13,1},{2,14},{6,10},... | collective-permute-start | bytes 995336 | tf_op jit(solution)/shard_map/ppermute | solution.py:53
  164.6 58.4 %collective-permute-start.9 = (bf16[288,576]{1,0:T(8,128)(2,1)}, bf16[288,576]{1,0:T(8,128)(2,1)}, u32[]{:S(2)}, u32[]{:S(2)}) collective-permute-start(bf16[288,576]{1,0:T(8,128)(2,1)} %get-tuple-element.12), channel_id=1, source_target_pairs={{0,8},{4,12},{8,0},{12,4},{1,9},{5,13},{9,1},{13,5},{2,10},{6,14},... | collective-permute-start | bytes 995336 | tf_op jit(solution)/shard_map/ppermute | solution.py:53
  166.8 57.8 %collective-permute-start.2 = (bf16[288,576]{1,0:T(8,128)(2,1)}, bf16[288,576]{1,0:T(8,128)(2,1)}, u32[]{:S(2)}, u32[]{:S(2)}) collective-permute-start(bf16[288,576]{1,0:T(8,128)(2,1)} %collective-permute-done.1), channel_id=1, source_target_pairs={{0,16},{16,0},{1,17},{17,1},{2,18},{18,2},{3,19},{19,3},{4,20},{20... | collective-permute-start | bytes 995336 | tf_op jit(solution)/shard_map/ppermute | solution.py:54
  179.0 49.6 %collective-permute-start.8 = (bf16[288,576]{1,0:T(8,128)(2,1)}, bf16[288,576]{1,0:T(8,128)(2,1)S(1)}, u32[]{:S(2)}, u32[]{:S(2)}) collective-permute-start(bf16[288,576]{1,0:T(8,128)(2,1)} %collective-permute-done.7), channel_id=1, source_target_pairs={{0,16},{16,0},{1,17},{17,1},{2,18},{18,2},{3,19},{19,3},{4,20},{20... | collective-permute-start | bytes 995336 | tf_op jit(solution)/shard_map/ppermute | solution.py:54
  210.8 32.5 %collective-permute-start.6 = (bf16[288,576]{1,0:T(8,128)(2,1)}, bf16[288,576]{1,0:T(8,128)(2,1)S(1)}, u32[]{:S(2)}, u32[]{:S(2)}) collective-permute-start(bf16[288,576]{1,0:T(8,128)(2,1)} %collective-permute-done.5), channel_id=1, source_target_pairs={{0,16},{16,0},{1,17},{17,1},{2,18},{18,2},{3,19},{19,3},{4,20},{20... | collective-permute-start | bytes 995336 | tf_op jit(solution)/shard_map/ppermute | solution.py:54
  211.3 19.9 %collective-permute-start.4 = (bf16[288,576]{1,0:T(8,128)(2,1)}, bf16[288,576]{1,0:T(8,128)(2,1)S(1)}, u32[]{:S(2)}, u32[]{:S(2)}) collective-permute-start(bf16[288,576]{1,0:T(8,128)(2,1)} %collective-permute-done.3), channel_id=1, source_target_pairs={{0,16},{16,0},{1,17},{17,1},{2,18},{18,2},{3,19},{19,3},{4,20},{20... | collective-permute-start | bytes 995336 | tf_op jit(solution)/shard_map/ppermute | solution.py:54
  223.1 21.1 %collective-permute-start.12 = (bf16[288,576]{1,0:T(8,128)(2,1)}, bf16[288,576]{1,0:T(8,128)(2,1)S(1)}, u32[]{:S(2)}, u32[]{:S(2)}) collective-permute-start(bf16[288,576]{1,0:T(8,128)(2,1)} %collective-permute-done.11), channel_id=1, source_target_pairs={{0,16},{16,0},{1,17},{17,1},{2,18},{18,2},{3,19},{19,3},{4,20},{20... | collective-permute-start | bytes 995336 | tf_op jit(solution)/shard_map/ppermute | solution.py:54
  224.5 16.3 %collective-permute-start.10 = (bf16[288,576]{1,0:T(8,128)(2,1)}, bf16[288,576]{1,0:T(8,128)(2,1)S(1)}, u32[]{:S(2)}, u32[]{:S(2)}) collective-permute-start(bf16[288,576]{1,0:T(8,128)(2,1)} %collective-permute-done.9), channel_id=1, source_target_pairs={{0,16},{16,0},{1,17},{17,1},{2,18},{18,2},{3,19},{19,3},{4,20},{20... | collective-permute-start | bytes 995336 | tf_op jit(solution)/shard_map/ppermute | solution.py:54
  280.9 112.1 %copy-start.5 = (f32[2304]{0:T(1024)S(1)}, f32[2304]{0:T(1024)}, u32[]{:S(2)}) copy-start(f32[2304]{0:T(1024)} %param.23) | copy-start | bytes 27652
  280.9 112.0 %collective-permute-start = (bf16[128,2304]{1,0:T(8,128)(2,1)S(1)}, bf16[128,2304]{1,0:T(8,128)(2,1)S(1)}, u32[]{:S(2)}, u32[]{:S(2)}) collective-permute-start(bf16[128,2304]{1,0:T(8,128)(2,1)S(1)} %get-tuple-element.6), channel_id=1, source_target_pairs={{0,0},{1,2},{2,1},{3,3},{4,4},{5,6},{6,5},{7,7},{8,8},{9,10},{10,9... | collective-permute-start | bytes 1769480 | tf_op jit(solution)/shard_map/ppermute | solution.py:171
  (4 other events, 104.4 us)
Sparse Core Ops, SparseCore 0:
  31.0 23.5 reduce-scatter.2
  58.5 150.1 all-gather.1
  281.0 110.5 reduce-scatter.4

commit v2 on v1

--- a/solution.py
+++ b/solution.py
@@ -38,14 +38,12 @@
     my_group = lax.axis_index("groups")
     piece = weight.shape[split_axis] // count
     depth = weight.shape[concat_axis]
-    shape = [piece, piece]
-    shape[concat_axis] = depth * count
     sizes = [piece, piece]
     sizes[concat_axis] = depth
     half = sizes[0] // groups
-    whole = jnp.zeros(shape, weight.dtype)
+    whole = jnp.zeros((count * sizes[0], sizes[1]), weight.dtype)
     own = lax.dynamic_slice_in_dim(weight, me * piece, piece, split_axis)
-    whole = lax.dynamic_update_slice_in_dim(whole, own, me * depth, concat_axis)
+    whole = lax.dynamic_update_slice_in_dim(whole, own, me * sizes[0], 0)
     for step in range(1, count):
         peer = me ^ step
         packet = lax.dynamic_slice_in_dim(weight, peer * piece, piece, split_axis)
@@ -53,9 +51,9 @@
         first = lax.ppermute(packet, "blk", [(i, i ^ step) for i in range(count)])
         second = lax.ppermute(first, "groups", [(0, 1), (1, 0)])
         for part, group in ((first, my_group), (second, 1 - my_group)):
-            at = [group * half, 0]
-            at[concat_axis] += peer * depth
-            whole = lax.dynamic_update_slice(whole, part, at)
+            whole = lax.dynamic_update_slice_in_dim(whole, part, peer * sizes[0] + group * half, 0)
+    if concat_axis == 1:
+        whole = whole.reshape(count, *sizes).transpose(1, 0, 2).reshape(sizes[0], count * sizes[1])
     return whole
 
 
@@ -160,8 +158,12 @@
     heads = lax.axis_size("heads")
     section_size = lax.axis_size("section")
     section_index = lax.axis_index("section")
-    attended = lax.psum_scatter(head_term, "heads", scatter_dimension=0, tiled=True).astype(jnp.float32)
-    out_rows = attended.shape[0]
+    swap = [(0, 1), (1, 0)]
+    out_rows = head_term.shape[0] // heads
+    own_term = lax.dynamic_slice_in_dim(head_term, head_index * out_rows, out_rows, 0)
+    sent_term = lax.dynamic_slice_in_dim(head_term, (1 - head_index) * out_rows, out_rows, 0)
+    other_term = lax.ppermute(sent_term, "heads", swap)
+    attended = own_term.astype(jnp.float32) + other_term.astype(jnp.float32)
     kept = lax.dynamic_slice_in_dim(dec_states, head_index * out_rows, out_rows, 0).astype(jnp.float32)
     residual = (kept + rms_scale(attended, post_attn_gain)).astype(jnp.bfloat16)
     ffn_input = rms_scale(residual.astype(jnp.float32), ffn_gain).astype(jnp.bfloat16)
@@ -169,14 +171,30 @@
         (h * section_size + s, s * heads + h) for h in range(heads) for s in range(section_size)
     ]
     residual_out = lax.ppermute(residual, ("heads", "section"), route)
-    ffn_rows = lax.all_gather(ffn_input, ("blk", "section", "heads"), axis=0, tiled=True)
-    gate = jnp.dot(ffn_rows, gate_mine, preferred_element_type=jnp.float32)
-    up_part = jnp.dot(ffn_rows, up_mine, preferred_element_type=jnp.float32)
-    hidden = (jax.nn.gelu(gate, approximate=True) * up_part).astype(jnp.bfloat16)
-    terms = jnp.dot(hidden, down_mine, preferred_element_type=jnp.float32).astype(jnp.bfloat16)
-    ffn_out = lax.psum_scatter(
-        terms, ("blk", "heads", "section"), scatter_dimension=0, tiled=True
-    ).astype(jnp.float32)
+    near = lax.all_gather(ffn_input, "blk", axis=0, tiled=True)
+    block_rows = near.shape[0]
+    mine = jnp.concatenate([near, lax.ppermute(near, "heads", swap)])
+    other = lax.ppermute(mine, "section", swap)
+    send_mine = section_index != head_index
+    kept_half = (section_index ^ head_index) * block_rows
+    sent_half = block_rows - kept_half
+
+    def summed_rows(rows):
+        gate = jnp.dot(rows, gate_mine, preferred_element_type=jnp.float32)
+        up_part = jnp.dot(rows, up_mine, preferred_element_type=jnp.float32)
+        hidden = (jax.nn.gelu(gate, approximate=True) * up_part).astype(jnp.bfloat16)
+        terms = jnp.dot(hidden, down_mine, preferred_element_type=jnp.float32).astype(jnp.bfloat16)
+        away = lax.ppermute(
+            lax.dynamic_slice_in_dim(terms, sent_half, block_rows, 0), "section", swap
+        )
+        here = lax.dynamic_slice_in_dim(terms, kept_half, block_rows, 0)
+        return here.astype(jnp.float32) + away.astype(jnp.float32)
+
+    first_sum = summed_rows(jnp.where(send_mine, mine, other)).astype(jnp.bfloat16)
+    arrived = lax.ppermute(first_sum, "heads", swap)
+    second_sum = summed_rows(jnp.where(send_mine, other, mine))
+    chip_sum = (second_sum + arrived.astype(jnp.float32)).astype(jnp.bfloat16)
+    ffn_out = lax.psum_scatter(chip_sum, "blk", scatter_dimension=0, tiled=True).astype(jnp.float32)
     return (residual_out.astype(jnp.float32) + rms_scale(ffn_out, post_ffn_gain)).astype(
         jnp.bfloat16
     )
@@ -191,7 +209,8 @@
     moved = 3 * width * units // blk + 2 * rows * width
     power = blk & (blk - 1) == 0
     fits = units % (blk * groups) == 0 and width % (blk * groups) == 0
-    return groups == 2 and power and fits and moved < gathered
+    pairs = groups == 2 and heads == 2 and section == 2
+    return pairs and power and fits and moved < gathered
 
 
 def solution(mesh):

time: 404 us -> 450 us (1.11)
  waiting for transfers between devices: 202 us -> 282 us
  starting transfers between devices: 49.8 us -> 25.1 us
  local copies, waits for them, and re-layouts: 69.4 us -> 53 us
    ppermute x0 -> x6, waiting for transfers between devices: none -> 112 us  [the longest x1 51.6 us: rows_body(): arrived = lax.ppermute(first_sum, 'heads', swap)]
    reduce_scatter x2 -> x1, waiting for transfers between devices: 134 us -> 46.6 us  [rows_body(): lax.psum_scatter(chip_sum, 'blk', scatter_dimension=0, tiled=True)]
    all_gather x1, waiting for transfers between devices: 0.01 us -> 50.2 us  [rows_body(): near = lax.all_gather(ffn_input, 'blk', axis=0, tiled=True)]
    dynamic_update_slice x21, local copies, waits for them, and re-layouts: 56.7 us -> 22.7 us  [the longest x18 18.6 us: reshard_over_blk(): lax.dynamic_update_slice_in_dim(whole, part, peer * sizes[0] + group * ha...]
    ppermute x9, starting transfers between devices: 38.3 us -> 8.65 us  [reshard_over_blk(): first = lax.ppermute(packet, 'blk', [(i, i ^ step) for i in range(count)])]
    unnamed x12 -> x37, local copies, waits for them, and re-layouts: 0.03 us -> 8.9 us
    ppermute x9, waiting for transfers between devices: 7.12 us -> 15.4 us  [reshard_over_blk(): second = lax.ppermute(first, 'groups', [(0, 1), (1, 0)])]
    dynamic_slice x0 -> x4, local copies, waits for them, and re-layouts: none -> 6.66 us  [the longest x2 5.1 us: summed_rows(): lax.dynamic_slice_in_dim(terms, sent_half, block_rows, 0)]
  transfers between devices with their start and end apart: 22 -> 27, of which waited for: 7 -> 13; matrix products, arithmetic and copies ran while one was open for 18% -> 16% of each run, Pallas kernels for 0% -> 0%
where the time goes in v2:
time: 450 us; the launch traced here: 449 us
  waiting for transfers between devices  282 us (63%)
  local copies, waits for them, and re-layouts  53 us (12%)
  matrix products  44 us (10%)
  starting transfers between devices  25.1 us (6%)
  blocking collectives  17.4 us (4%)
  between operations  13.7 us (3%)
  other arithmetic  13.3 us (3%)
    ppermute x9, waiting for transfers between devices, reshard_over_blk(): first = lax.ppermute(packet, 'blk', [(i, i ^ step) for i in range(count)])  58 us
    ppermute x1, waiting for transfers between devices, rows_body(): arrived = lax.ppermute(first_sum, 'heads', swap)  51.6 us
    all_gather x1, waiting for transfers between devices, rows_body(): near = lax.all_gather(ffn_input, 'blk', axis=0, tiled=True)  50.2 us
    ppermute x1, waiting for transfers between devices, rows_body(): mine = jnp.concatenate([near, lax.ppermute(near, 'heads', swap)])  48.5 us
    reduce_scatter x1, waiting for transfers between devices, rows_body(): lax.psum_scatter(chip_sum, 'blk', scatter_dimension=0, tiled=True)  46.6 us
    dot_general x2, matrix products, summed_rows(): jnp.dot(hidden, down_mine, preferred_element_type=jnp.float32)  25.7 us
    dynamic_update_slice x18, local copies, waits for them, and re-layouts, reshard_over_blk(): lax.dynamic_update_slice_in_dim(whole, part, peer * sizes[0] + group * ha...  18.6 us
    all_gather x1, blocking collectives, rows_body(): lax.all_gather(jnp.stack([keys_local, values_local]), 'blk', axis=1, tile...  17.4 us
  transfers between devices with their start and end apart: 27, of which 13 were waited for; matrix products, arithmetic and copies ran while one was open for 16% of the time, Pallas kernels for 0%

profile of v2, /device:TPU:0, one launch (start us, length us, event | category | flops | bytes accessed | tf_op | source)
XLA Modules:
  0.0 448.8 jit_solution(16935226367137601208)
XLA Ops:
  9.1 17.4 %all_gather.6 = bf16[2,512,256]{2,1,0:T(8,128)(2,1)S(1)} all-gather(bf16[2,128,256]{2,1,0:T(8,128)(2,1)S(1)} %pad_maximum_fusion), channel_id=1, replica_groups=mesh['groups'=2,'blk'=4,'heads'=2,'section'=2] {'blk'}, dimensions={1}, use_global_device_ids=true | all-gather | bytes 655360 | tf_op jit(solution)/shard_map/all_gather | solution.py:146
  27.3 3.2 fusion.58
  33.9 12.1 %collective-permute-done = bf16[128,2304]{1,0:T(8,128)(2,1)S(1)} collective-permute-done((bf16[128,2304]{1,0:T(8,128)(2,1)S(1)}, bf16[128,2304]{1,0:T(8,128)(2,1)S(1)}, u32[]{:S(2)}, u32[]{:S(2)}) %collective-permute-start) | collective-permute-done | bytes 589856 | tf_op jit(solution)/shard_map/ppermute | solution.py:165
  48.7 50.2 %all-gather.2.cloned.1.call-done = bf16[512,2304]{1,0:T(8,128)(2,1)} async-done(((bf16[128,2304]{1,0:T(8,128)(2,1)}), bf16[512,2304]{1,0:T(8,128)(2,1)}) %all-gather.2.cloned.1.call-update) | async-done | bytes 2359312 | tf_op jit(solution)/shard_map/all_gather | solution.py:174
  100.4 3.2 constant_dynamic-update-slice_fusion.20
  103.6 48.5 %collective-permute-done.2 = bf16[512,2304]{1,0:T(8,128)(2,1)S(1)} collective-permute-done((bf16[512,2304]{1,0:T(8,128)(2,1)}, bf16[512,2304]{1,0:T(8,128)(2,1)S(1)}, u32[]{:S(2)}, u32[]{:S(2)}) %collective-permute-start.2) | collective-permute-done | bytes 2359328 | tf_op jit(solution)/shard_map/ppermute | solution.py:176
  153.6 3.0 fusion.57
  156.6 2.9 fusion.56
  179.9 11.8 %collective-permute-done.16 = bf16[288,576]{1,0:T(8,128)(2,1)} collective-permute-done((bf16[288,576]{1,0:T(8,128)(2,1)}, bf16[288,576]{1,0:T(8,128)(2,1)}, u32[]{:S(2)}, u32[]{:S(2)}) %collective-permute-start.16) | collective-permute-done | bytes 331808 | tf_op jit(solution)/shard_map/ppermute | solution.py:51
  198.0 2.6 collective-permute-done.20
  205.9 5.3 %collective-permute-done.19 = bf16[288,576]{1,0:T(8,128)(2,1)S(1)} collective-permute-done((bf16[288,576]{1,0:T(8,128)(2,1)}, bf16[288,576]{1,0:T(8,128)(2,1)S(1)}, u32[]{:S(2)}, u32[]{:S(2)}) %collective-permute-start.19) | collective-permute-done | bytes 331808 | tf_op jit(solution)/shard_map/ppermute | solution.py:52
  212.5 16.9 %collective-permute-done.6 = bf16[288,576]{1,0:T(8,128)(2,1)} collective-permute-done((bf16[288,576]{1,0:T(8,128)(2,1)S(1)}, bf16[288,576]{1,0:T(8,128)(2,1)}, u32[]{:S(2)}, u32[]{:S(2)}) %collective-permute-start.6) | collective-permute-done | bytes 331808 | tf_op jit(solution)/shard_map/ppermute | solution.py:51
  232.1 3.1 copy.45
  239.3 3.7 collective-permute-done.14
  244.3 23.0 %collective-permute-done.12 = bf16[288,576]{1,0:T(8,128)(2,1)} collective-permute-done((bf16[288,576]{1,0:T(8,128)(2,1)S(1)}, bf16[288,576]{1,0:T(8,128)(2,1)}, u32[]{:S(2)}, u32[]{:S(2)}) %collective-permute-start.12) | collective-permute-done | bytes 331808 | tf_op jit(solution)/shard_map/ppermute | solution.py:51
  275.6 8.7 %collective-permute-done.13 = bf16[288,576]{1,0:T(8,128)(2,1)S(1)} collective-permute-done((bf16[288,576]{1,0:T(8,128)(2,1)}, bf16[288,576]{1,0:T(8,128)(2,1)S(1)}, u32[]{:S(2)}, u32[]{:S(2)}) %collective-permute-start.13) | collective-permute-done | bytes 331808 | tf_op jit(solution)/shard_map/ppermute | solution.py:52
  287.8 6.7 %fusion.24 = f32[1024,576]{0,1:T(8,128)} fusion(bf16[2304,576]{1,0:T(8,128)(2,1)S(1)} %constant_dynamic-update-slice_fusion.13, bf16[1024,2304]{1,0:T(8,128)(2,1)} %constant_dynamic-update-slice_fusion.19, bf16[1024,2304]{1,0:T(8,128)(2,1)} %collective-permute-done.3, pred[]{:T(512)S(6)} %ne.7), kind=kOutput, calls=%fused_computation.35 | convolution fusion | flops 2720268288 | bytes 14450689 | tf_op jit(solution)/shard_map/dot_general | solution.py:183
  294.5 12.9 %convolution_convert_fusion = bf16[1024,2304]{1,0:T(8,128)(2,1)} fusion(bf16[576,2304]{0,1:T(8,128)(2,1)} %bitcast.25, f32[1024,576]{0,1:T(8,128)} %fusion.24, bf16[2304,576]{1,0:T(8,128)(2,1)} %constant_dynamic-update-slice_fusion.7, bf16[1024,2304]{1,0:T(8,128)(2,1)} %constant_dynamic-update-slice_fusion.19, bf16[1024,2304]{1,0:T(8,128)(2,1)} %collective-permute-done.3, ...), kind=kOutput, calls=%fused_computation | convolution fusion | flops 5446434816 | bytes 21823488 | tf_op jit(solution)/shard_map/dot_general | solution.py:186
  307.3 3.3 constant_dynamic-slice_fusion.5
  310.6 6.7 %fusion.22 = f32[1024,576]{0,1:T(8,128)} fusion(bf16[2304,576]{1,0:T(8,128)(2,1)S(1)} %constant_dynamic-update-slice_fusion.13, bf16[1024,2304]{1,0:T(8,128)(2,1)} %collective-permute-done.3, bf16[1024,2304]{1,0:T(8,128)(2,1)} %constant_dynamic-update-slice_fusion.19, pred[]{:T(512)S(6)} %ne.7), kind=kOutput, calls=%fused_computation.33 | convolution fusion | flops 2720268288 | bytes 14450689 | tf_op jit(solution)/shard_map/dot_general | solution.py:183
  317.3 12.8 %convolution_convert_fusion.1 = bf16[1024,2304]{1,0:T(8,128)(2,1)} fusion(bf16[576,2304]{0,1:T(8,128)(2,1)} %bitcast.26, f32[1024,576]{0,1:T(8,128)} %fusion.22, bf16[2304,576]{1,0:T(8,128)(2,1)} %constant_dynamic-update-slice_fusion.7, bf16[1024,2304]{1,0:T(8,128)(2,1)} %collective-permute-done.3, ...), kind=kOutput, calls=%fused_computation.1 | convolution fusion | flops 5446434816 | bytes 21823488 | tf_op jit(solution)/shard_map/dot_general | solution.py:186
  332.5 3.2 add_convert_fusion.1
  337.3 51.6 %collective-permute-done.24 = bf16[512,2304]{1,0:T(8,128)(2,1)S(1)} collective-permute-done((bf16[512,2304]{1,0:T(8,128)(2,1)S(1)}, bf16[512,2304]{1,0:T(8,128)(2,1)S(1)}, u32[]{:S(2)}, u32[]{:S(2)}) %collective-permute-start.24) | collective-permute-done | bytes 2359328 | tf_op jit(solution)/shard_map/ppermute | solution.py:194
  391.9 46.6 %reduce-scatter.2.cloned.1.call-done = bf16[128,2304]{1,0:T(8,128)(2,1)} async-done(((bf16[512,2304]{1,0:T(8,128)(2,1)}), bf16[128,2304]{1,0:T(8,128)(2,1)}) %reduce-scatter.2.cloned.1.call-update) | async-done | bytes 589840 | tf_op jit(solution)/shard_map/reduce_scatter | solution.py:197
  (122 shorter events, 76.0 us)
Async XLA Ops:
  6.5 92.4 %all-gather.2.cloned.1.call-start = ((), (), s32[]{:S(2)}) async-start(), calls=%async_computation.1 | async-start | bytes 2949120 | tf_op jit(solution)/shard_map/all_gather | solution.py:174
  32.3 13.7 %collective-permute-start = (bf16[128,2304]{1,0:T(8,128)(2,1)S(1)}, bf16[128,2304]{1,0:T(8,128)(2,1)S(1)}, u32[]{:S(2)}, u32[]{:S(2)}) collective-permute-start(bf16[128,2304]{1,0:T(8,128)(2,1)S(1)} %constant_dynamic-slice_fusion.6), channel_id=1, source_target_pairs={{0,2},{2,0},{1,3},{3,1},{4,6},{6,4},{5,7},{7,5},{8,10},{10,8},{9,1... | collective-permute-start | bytes 1769480 | tf_op jit(solution)/shard_map/ppermute | solution.py:165
  48.7 389.8 %reduce-scatter.2.cloned.1.call-start = ((), (), s32[]{:S(2)}) async-start(), calls=%async_computation.2 | async-start | bytes 2949120 | tf_op jit(solution)/shard_map/reduce_scatter | solution.py:197
  98.9 53.2 %collective-permute-start.2 = (bf16[512,2304]{1,0:T(8,128)(2,1)}, bf16[512,2304]{1,0:T(8,128)(2,1)S(1)}, u32[]{:S(2)}, u32[]{:S(2)}) collective-permute-start(bf16[512,2304]{1,0:T(8,128)(2,1)} %all-gather.2.cloned.1.call-done), channel_id=1, source_target_pairs={{0,2},{2,0},{1,3},{3,1},{4,6},{6,4},{5,7},{7,5},{8,10},{10,8},{9,1... | collective-permute-start | bytes 7077896 | tf_op jit(solution)/shard_map/ppermute | solution.py:176
  153.6 134.2 %collective-permute-start.3 = (bf16[1024,2304]{1,0:T(8,128)(2,1)}, bf16[1024,2304]{1,0:T(8,128)(2,1)}, u32[]{:S(2)}, u32[]{:S(2)}) collective-permute-start(bf16[1024,2304]{1,0:T(8,128)(2,1)} %constant_dynamic-update-slice_fusion.19), channel_id=1, source_target_pairs={{0,1},{1,0},{2,3},{3,2},{4,5},{5,4},{6,7},{7,6},{8,9},{9,8},{10,11... | collective-permute-start | bytes 14155784 | tf_op jit(solution)/shard_map/ppermute | solution.py:177
  156.6 20.6 %collective-permute-start.4 = (bf16[288,576]{1,0:T(8,128)(2,1)}, bf16[288,576]{1,0:T(8,128)(2,1)}, u32[]{:S(2)}, u32[]{:S(2)}) collective-permute-start(bf16[288,576]{1,0:T(8,128)(2,1)} %get-tuple-element.11), channel_id=1, source_target_pairs={{0,4},{4,0},{8,12},{12,8},{1,5},{5,1},{9,13},{13,9},{2,6},{6,2},{1... | collective-permute-start | bytes 995336 | tf_op jit(solution)/shard_map/ppermute | solution.py:51
  159.5 35.7 %collective-permute-start.10 = (bf16[288,576]{1,0:T(8,128)(2,1)}, bf16[288,576]{1,0:T(8,128)(2,1)}, u32[]{:S(2)}, u32[]{:S(2)}) collective-permute-start(bf16[288,576]{1,0:T(8,128)(2,1)} %get-tuple-element.8), channel_id=1, source_target_pairs={{0,4},{4,0},{8,12},{12,8},{1,5},{5,1},{9,13},{13,9},{2,6},{6,2},{1... | collective-permute-start | bytes 995336 | tf_op jit(solution)/shard_map/ppermute | solution.py:51
  164.4 27.2 %collective-permute-start.16 = (bf16[288,576]{1,0:T(8,128)(2,1)}, bf16[288,576]{1,0:T(8,128)(2,1)}, u32[]{:S(2)}, u32[]{:S(2)}) collective-permute-start(bf16[288,576]{1,0:T(8,128)(2,1)} %copy.47), channel_id=1, source_target_pairs={{0,4},{4,0},{8,12},{12,8},{1,5},{5,1},{9,13},{13,9},{2,6},{6,2},{1... | collective-permute-start | bytes 995336 | tf_op jit(solution)/shard_map/ppermute | solution.py:51
  165.4 29.9 %collective-permute-start.18 = (bf16[288,576]{1,0:T(8,128)(2,1)}, bf16[288,576]{1,0:T(8,128)(2,1)}, u32[]{:S(2)}, u32[]{:S(2)}) collective-permute-start(bf16[288,576]{1,0:T(8,128)(2,1)} %copy.48), channel_id=1, source_target_pairs={{0,8},{4,12},{8,0},{12,4},{1,9},{5,13},{9,1},{13,5},{2,10},{6,14},... | collective-permute-start | bytes 995336 | tf_op jit(solution)/shard_map/ppermute | solution.py:51
  177.2 23.4 %collective-permute-start.20 = (bf16[288,576]{1,0:T(8,128)(2,1)S(1)}, bf16[288,576]{1,0:T(8,128)(2,1)S(1)}, u32[]{:S(2)}, u32[]{:S(2)}) collective-permute-start(bf16[288,576]{1,0:T(8,128)(2,1)S(1)} %copy-done.12), channel_id=1, source_target_pairs={{0,12},{4,8},{8,4},{12,0},{1,13},{5,9},{9,5},{13,1},{2,14},{6,10},... | collective-permute-start | bytes 995336 | tf_op jit(solution)/shard_map/ppermute | solution.py:51
  195.3 34.2 %collective-permute-start.6 = (bf16[288,576]{1,0:T(8,128)(2,1)S(1)}, bf16[288,576]{1,0:T(8,128)(2,1)}, u32[]{:S(2)}, u32[]{:S(2)}) collective-permute-start(bf16[288,576]{1,0:T(8,128)(2,1)S(1)} %copy-done.10), channel_id=1, source_target_pairs={{0,8},{4,12},{8,0},{12,4},{1,9},{5,13},{9,1},{13,5},{2,10},{6,14},... | collective-permute-start | bytes 995336 | tf_op jit(solution)/shard_map/ppermute | solution.py:51
  195.3 15.9 %collective-permute-start.19 = (bf16[288,576]{1,0:T(8,128)(2,1)}, bf16[288,576]{1,0:T(8,128)(2,1)S(1)}, u32[]{:S(2)}, u32[]{:S(2)}) collective-permute-start(bf16[288,576]{1,0:T(8,128)(2,1)} %collective-permute-done.18), channel_id=1, source_target_pairs={{0,16},{16,0},{1,17},{17,1},{2,18},{18,2},{3,19},{19,3},{4,20},{20... | collective-permute-start | bytes 995336 | tf_op jit(solution)/shard_map/ppermute | solution.py:52
  200.6 29.9 %collective-permute-start.5 = (bf16[288,576]{1,0:T(8,128)(2,1)}, bf16[288,576]{1,0:T(8,128)(2,1)S(1)}, u32[]{:S(2)}, u32[]{:S(2)}) collective-permute-start(bf16[288,576]{1,0:T(8,128)(2,1)} %collective-permute-done.4), channel_id=1, source_target_pairs={{0,16},{16,0},{1,17},{17,1},{2,18},{18,2},{3,19},{19,3},{4,20},{20... | collective-permute-start | bytes 995336 | tf_op jit(solution)/shard_map/ppermute | solution.py:52
  203.3 27.2 %collective-permute-start.21 = (bf16[288,576]{1,0:T(8,128)(2,1)S(1)}, bf16[288,576]{1,0:T(8,128)(2,1)S(1)}, u32[]{:S(2)}, u32[]{:S(2)}) collective-permute-start(bf16[288,576]{1,0:T(8,128)(2,1)S(1)} %collective-permute-done.20), channel_id=1, source_target_pairs={{0,16},{16,0},{1,17},{17,1},{2,18},{18,2},{3,19},{19,3},{4,20},{20... | collective-permute-start | bytes 995336 | tf_op jit(solution)/shard_map/ppermute | solution.py:52
  211.2 25.6 %collective-permute-start.8 = (bf16[288,576]{1,0:T(8,128)(2,1)}, bf16[288,576]{1,0:T(8,128)(2,1)}, u32[]{:S(2)}, u32[]{:S(2)}) collective-permute-start(bf16[288,576]{1,0:T(8,128)(2,1)} %get-tuple-element.10), channel_id=1, source_target_pairs={{0,12},{4,8},{8,4},{12,0},{1,13},{5,9},{9,5},{13,1},{2,14},{6,10},... | collective-permute-start | bytes 995336 | tf_op jit(solution)/shard_map/ppermute | solution.py:51
  230.5 36.8 %collective-permute-start.12 = (bf16[288,576]{1,0:T(8,128)(2,1)S(1)}, bf16[288,576]{1,0:T(8,128)(2,1)}, u32[]{:S(2)}, u32[]{:S(2)}) collective-permute-start(bf16[288,576]{1,0:T(8,128)(2,1)S(1)} %get-tuple-element.9), channel_id=1, source_target_pairs={{0,8},{4,12},{8,0},{12,4},{1,9},{5,13},{9,1},{13,5},{2,10},{6,14},... | collective-permute-start | bytes 995336 | tf_op jit(solution)/shard_map/ppermute | solution.py:51
  230.5 38.2 %collective-permute-start.7 = (bf16[288,576]{1,0:T(8,128)(2,1)}, bf16[288,576]{1,0:T(8,128)(2,1)}, u32[]{:S(2)}, u32[]{:S(2)}) collective-permute-start(bf16[288,576]{1,0:T(8,128)(2,1)} %collective-permute-done.6), channel_id=1, source_target_pairs={{0,16},{16,0},{1,17},{17,1},{2,18},{18,2},{3,19},{19,3},{4,20},{20... | collective-permute-start | bytes 995336 | tf_op jit(solution)/shard_map/ppermute | solution.py:52
  236.9 36.0 %collective-permute-start.11 = (bf16[288,576]{1,0:T(8,128)(2,1)}, bf16[288,576]{1,0:T(8,128)(2,1)S(1)}, u32[]{:S(2)}, u32[]{:S(2)}) collective-permute-start(bf16[288,576]{1,0:T(8,128)(2,1)} %collective-permute-done.10), channel_id=1, source_target_pairs={{0,16},{16,0},{1,17},{17,1},{2,18},{18,2},{3,19},{19,3},{4,20},{20... | collective-permute-start | bytes 995336 | tf_op jit(solution)/shard_map/ppermute | solution.py:52
  242.9 44.0 %collective-permute-start.9 = (bf16[288,576]{1,0:T(8,128)(2,1)}, bf16[288,576]{1,0:T(8,128)(2,1)S(1)}, u32[]{:S(2)}, u32[]{:S(2)}) collective-permute-start(bf16[288,576]{1,0:T(8,128)(2,1)} %collective-permute-done.8), channel_id=1, source_target_pairs={{0,16},{16,0},{1,17},{17,1},{2,18},{18,2},{3,19},{19,3},{4,20},{20... | collective-permute-start | bytes 995336 | tf_op jit(solution)/shard_map/ppermute | solution.py:52
  267.3 19.7 %collective-permute-start.15 = (bf16[288,576]{1,0:T(8,128)(2,1)}, bf16[288,576]{1,0:T(8,128)(2,1)S(1)}, u32[]{:S(2)}, u32[]{:S(2)}) collective-permute-start(bf16[288,576]{1,0:T(8,128)(2,1)} %collective-permute-done.14), channel_id=1, source_target_pairs={{0,16},{16,0},{1,17},{17,1},{2,18},{18,2},{3,19},{19,3},{4,20},{20... | collective-permute-start | bytes 995336 | tf_op jit(solution)/shard_map/ppermute | solution.py:52
  268.7 15.7 %collective-permute-start.13 = (bf16[288,576]{1,0:T(8,128)(2,1)}, bf16[288,576]{1,0:T(8,128)(2,1)S(1)}, u32[]{:S(2)}, u32[]{:S(2)}) collective-permute-start(bf16[288,576]{1,0:T(8,128)(2,1)} %collective-permute-done.12), channel_id=1, source_target_pairs={{0,16},{16,0},{1,17},{17,1},{2,18},{18,2},{3,19},{19,3},{4,20},{20... | collective-permute-start | bytes 995336 | tf_op jit(solution)/shard_map/ppermute | solution.py:52
  310.6 21.9 %collective-permute-start.23 = (bf16[512,2304]{1,0:T(8,128)(2,1)}, bf16[512,2304]{1,0:T(8,128)(2,1)}, u32[]{:S(2)}, u32[]{:S(2)}) collective-permute-start(bf16[512,2304]{1,0:T(8,128)(2,1)} %constant_dynamic-slice_fusion.5), channel_id=1, source_target_pairs={{0,1},{1,0},{2,3},{3,2},{4,5},{5,4},{6,7},{7,6},{8,9},{9,8},{10,11... | collective-permute-start | bytes 7077896 | tf_op jit(solution)/shard_map/ppermute | solution.py:187
  335.7 53.1 %collective-permute-start.24 = (bf16[512,2304]{1,0:T(8,128)(2,1)S(1)}, bf16[512,2304]{1,0:T(8,128)(2,1)S(1)}, u32[]{:S(2)}, u32[]{:S(2)}) collective-permute-start(bf16[512,2304]{1,0:T(8,128)(2,1)S(1)} %add_convert_fusion.1), channel_id=1, source_target_pairs={{0,2},{2,0},{1,3},{3,1},{4,6},{6,4},{5,7},{7,5},{8,10},{10,8},{9,1... | collective-permute-start | bytes 7077896 | tf_op jit(solution)/shard_map/ppermute | solution.py:194
  391.2 48.6 %collective-permute-start.1 = (bf16[128,2304]{1,0:T(8,128)(2,1)S(1)}, bf16[128,2304]{1,0:T(8,128)(2,1)S(1)}, u32[]{:S(2)}, u32[]{:S(2)}) collective-permute-start(bf16[128,2304]{1,0:T(8,128)(2,1)S(1)} %copy-done.8), channel_id=1, source_target_pairs={{0,0},{1,2},{2,1},{3,3},{4,4},{5,6},{6,5},{7,7},{8,8},{9,10},{10,9... | collective-permute-start | bytes 1769480 | tf_op jit(solution)/shard_map/ppermute | solution.py:173
  (19 other events, 392.1 us)
Sparse Core Ops, SparseCore 0:
  48.8 50.0 all-gather.1
  391.3 47.1 reduce-scatter.1

commit v3 on v1

--- a/solution.py
+++ b/solution.py
@@ -38,14 +38,12 @@
     my_group = lax.axis_index("groups")
     piece = weight.shape[split_axis] // count
     depth = weight.shape[concat_axis]
-    shape = [piece, piece]
-    shape[concat_axis] = depth * count
     sizes = [piece, piece]
     sizes[concat_axis] = depth
     half = sizes[0] // groups
-    whole = jnp.zeros(shape, weight.dtype)
+    whole = jnp.zeros((count * sizes[0], sizes[1]), weight.dtype)
     own = lax.dynamic_slice_in_dim(weight, me * piece, piece, split_axis)
-    whole = lax.dynamic_update_slice_in_dim(whole, own, me * depth, concat_axis)
+    whole = lax.dynamic_update_slice_in_dim(whole, own, me * sizes[0], 0)
     for step in range(1, count):
         peer = me ^ step
         packet = lax.dynamic_slice_in_dim(weight, peer * piece, piece, split_axis)
@@ -53,9 +51,9 @@
         first = lax.ppermute(packet, "blk", [(i, i ^ step) for i in range(count)])
         second = lax.ppermute(first, "groups", [(0, 1), (1, 0)])
         for part, group in ((first, my_group), (second, 1 - my_group)):
-            at = [group * half, 0]
-            at[concat_axis] += peer * depth
-            whole = lax.dynamic_update_slice(whole, part, at)
+            whole = lax.dynamic_update_slice_in_dim(whole, part, peer * sizes[0] + group * half, 0)
+    if concat_axis == 1:
+        whole = whole.reshape(count, *sizes).transpose(1, 0, 2).reshape(sizes[0], count * sizes[1])
     return whole
 
 
@@ -160,8 +158,12 @@
     heads = lax.axis_size("heads")
     section_size = lax.axis_size("section")
     section_index = lax.axis_index("section")
-    attended = lax.psum_scatter(head_term, "heads", scatter_dimension=0, tiled=True).astype(jnp.float32)
-    out_rows = attended.shape[0]
+    swap = [(0, 1), (1, 0)]
+    out_rows = head_term.shape[0] // heads
+    own_term = lax.dynamic_slice_in_dim(head_term, head_index * out_rows, out_rows, 0)
+    sent_term = lax.dynamic_slice_in_dim(head_term, (1 - head_index) * out_rows, out_rows, 0)
+    other_term = lax.ppermute(sent_term, "heads", swap)
+    attended = own_term.astype(jnp.float32) + other_term.astype(jnp.float32)
     kept = lax.dynamic_slice_in_dim(dec_states, head_index * out_rows, out_rows, 0).astype(jnp.float32)
     residual = (kept + rms_scale(attended, post_attn_gain)).astype(jnp.bfloat16)
     ffn_input = rms_scale(residual.astype(jnp.float32), ffn_gain).astype(jnp.bfloat16)
@@ -191,7 +193,8 @@
     moved = 3 * width * units // blk + 2 * rows * width
     power = blk & (blk - 1) == 0
     fits = units % (blk * groups) == 0 and width % (blk * groups) == 0
-    return groups == 2 and power and fits and moved < gathered
+    pairs = groups == 2 and heads == 2 and section == 2
+    return pairs and power and fits and moved < gathered
 
 
 def solution(mesh):

time: 404 us -> 401 us (level)
  waiting for transfers between devices: 202 us -> 243 us
  starting transfers between devices: 49.8 us -> 21.6 us
  local copies, waits for them, and re-layouts: 69.4 us -> 53.7 us
    ppermute x9, waiting for transfers between devices: 60.9 us -> 107 us  [reshard_over_blk(): first = lax.ppermute(packet, 'blk', [(i, i ^ step) for i in range(count)])]
    dynamic_update_slice x21, local copies, waits for them, and re-layouts: 56.7 us -> 27.6 us  [the longest x18 21.9 us: reshard_over_blk(): lax.dynamic_update_slice_in_dim(whole, part, peer * sizes[0] + group * ha...]
    ppermute x9, starting transfers between devices: 38.3 us -> 9.88 us  [reshard_over_blk(): first = lax.ppermute(packet, 'blk', [(i, i ^ step) for i in range(count)])]
    reduce_scatter x1 -> x0, waiting for transfers between devices: 23.6 us -> none  [rows_body(): lax.psum_scatter(head_term, 'heads', scatter_dimension=0, tiled=True)]
    ppermute x0 -> x1, waiting for transfers between devices: none -> 12.5 us  [rows_body(): other_term = lax.ppermute(sent_term, 'heads', swap)]
    ppermute x9, waiting for transfers between devices: 7.12 us -> 13.9 us  [reshard_over_blk(): second = lax.ppermute(first, 'groups', [(0, 1), (1, 0)])]
    unnamed x12 -> x24, local copies, waits for them, and re-layouts: 0.03 us -> 5.93 us
    transpose x0 -> x1, local copies, waits for them, and re-layouts: none -> 4.6 us  [reshard_over_blk(): whole.reshape(count, *sizes).transpose(1, 0, 2)]
  transfers between devices with their start and end apart: 22 -> 22, of which waited for: 7 -> 7; matrix products, arithmetic and copies ran while one was open for 18% -> 13% of each run, Pallas kernels for 0% -> 0%
where the time goes in v3:
time: 401 us; the launch traced here: 400 us
  waiting for transfers between devices  243 us (61%)
  local copies, waits for them, and re-layouts  53.7 us (13%)
  matrix products  40.9 us (10%)
  starting transfers between devices  21.6 us (5%)
  blocking collectives  17.4 us (4%)
  between operations  13.6 us (3%)
  other arithmetic  9.93 us (2%)
    reduce_scatter x1, waiting for transfers between devices, rows_body(): lax.psum_scatter(terms, ('blk', 'heads', 'section'), scatter_dimension=0,...  110 us
    ppermute x9, waiting for transfers between devices, reshard_over_blk(): first = lax.ppermute(packet, 'blk', [(i, i ^ step) for i in range(count)])  107 us
    dot_general x1, matrix products, rows_body(): jnp.dot(hidden, down_mine, preferred_element_type=jnp.float32)  25.3 us
    dynamic_update_slice x18, local copies, waits for them, and re-layouts, reshard_over_blk(): lax.dynamic_update_slice_in_dim(whole, part, peer * sizes[0] + group * ha...  21.9 us
    all_gather x1, blocking collectives, rows_body(): lax.all_gather(jnp.stack([keys_local, values_local]), 'blk', axis=1, tile...  17.4 us
    ppermute x9, waiting for transfers between devices, reshard_over_blk(): second = lax.ppermute(first, 'groups', [(0, 1), (1, 0)])  13.9 us
    ppermute x1, waiting for transfers between devices, rows_body(): other_term = lax.ppermute(sent_term, 'heads', swap)  12.5 us
    dot_general x1, matrix products, rows_body(): gate = jnp.dot(ffn_rows, gate_mine, preferred_element_type=jnp.float32)  10.6 us
  transfers between devices with their start and end apart: 22, of which 7 were waited for; matrix products, arithmetic and copies ran while one was open for 13% of the time, Pallas kernels for 0%

profile of v3, /device:TPU:0, one launch (start us, length us, event | category | flops | bytes accessed | tf_op | source)
XLA Modules:
  0.0 400.1 jit_solution(4147767315165437933)
XLA Ops:
  9.1 17.4 %all_gather.6 = bf16[2,512,256]{2,1,0:T(8,128)(2,1)S(1)} all-gather(bf16[2,128,256]{2,1,0:T(8,128)(2,1)S(1)} %pad_maximum_fusion), channel_id=1, replica_groups=mesh['groups'=2,'blk'=4,'heads'=2,'section'=2] {'blk'}, dimensions={1}, use_global_device_ids=true | all-gather | bytes 655360 | tf_op jit(solution)/shard_map/all_gather | solution.py:146
  27.3 3.2 fusion.46
  30.5 1.8 convolution_convert_fusion.1
  34.6 12.5 %collective-permute-done = bf16[128,2304]{1,0:T(8,128)(2,1)} collective-permute-done((bf16[128,2304]{1,0:T(8,128)(2,1)}, bf16[128,2304]{1,0:T(8,128)(2,1)}, u32[]{:S(2)}, u32[]{:S(2)}) %collective-permute-start) | collective-permute-done | bytes 589856 | tf_op jit(solution)/shard_map/ppermute | solution.py:165
  52.0 2.9 fusion.44
  54.9 2.7 fusion.45
  57.6 2.0 collective-permute-start.8
  59.6 2.1 constant_dynamic-slice_fusion
  63.7 2.5 collective-permute-start.16
  70.9 1.8 broadcast.67.clone.1
  72.7 2.4 dynamic-slice_dynamic-update-slice_fusion.1
  75.1 1.8 broadcast.67.clone.2
  77.0 2.4 dynamic-slice_dynamic-update-slice_fusion
  82.1 26.5 %collective-permute-done.14 = bf16[288,576]{1,0:T(8,128)(2,1)} collective-permute-done((bf16[288,576]{1,0:T(8,128)(2,1)}, bf16[288,576]{1,0:T(8,128)(2,1)}, u32[]{:S(2)}, u32[]{:S(2)}) %collective-permute-start.14) | collective-permute-done | bytes 331808 | tf_op jit(solution)/shard_map/ppermute | solution.py:51
  116.9 7.0 %collective-permute-done.18 = bf16[288,576]{1,0:T(8,128)(2,1)} collective-permute-done((bf16[288,576]{1,0:T(8,128)(2,1)}, bf16[288,576]{1,0:T(8,128)(2,1)}, u32[]{:S(2)}, u32[]{:S(2)}) %collective-permute-start.18) | collective-permute-done | bytes 331808 | tf_op jit(solution)/shard_map/ppermute | solution.py:51
  123.9 2.6 collective-permute-start.12
  130.4 58.6 %collective-permute-done.4 = bf16[288,576]{1,0:T(8,128)(2,1)} collective-permute-done((bf16[288,576]{1,0:T(8,128)(2,1)S(1)}, bf16[288,576]{1,0:T(8,128)(2,1)}, u32[]{:S(2)}, u32[]{:S(2)}) %collective-permute-start.4) | collective-permute-done | bytes 331808 | tf_op jit(solution)/shard_map/ppermute | solution.py:51
  194.3 4.6 %copy.45 = bf16[576,4,576]{0,2,1:T(8,128)(2,1)} copy(bf16[576,4,576]{2,0,1:T(8,128)(2,1)} %bitcast.5) | data formatting | bytes 5308416 | tf_op jit(solution)/shard_map/transpose | solution.py:56
  201.0 14.6 %collective-permute-done.10 = bf16[288,576]{1,0:T(8,128)(2,1)S(1)} collective-permute-done((bf16[288,576]{1,0:T(8,128)(2,1)S(1)}, bf16[288,576]{1,0:T(8,128)(2,1)S(1)}, u32[]{:S(2)}, u32[]{:S(2)}) %collective-permute-start.10) | collective-permute-done | bytes 331808 | tf_op jit(solution)/shard_map/ppermute | solution.py:51
  225.2 13.9 %collective-permute-done.11 = bf16[288,576]{1,0:T(8,128)(2,1)S(1)} collective-permute-done((bf16[288,576]{1,0:T(8,128)(2,1)S(1)}, bf16[288,576]{1,0:T(8,128)(2,1)S(1)}, u32[]{:S(2)}, u32[]{:S(2)}) %collective-permute-start.11) | collective-permute-done | bytes 331808 | tf_op jit(solution)/shard_map/ppermute | solution.py:52
  242.1 10.6 %fusion.51 = f32[2048,576]{0,1:T(8,128)} fusion(bf16[2048,2304]{1,0:T(8,128)(2,1)} %all-gather.2.cloned.1.call-done, bf16[2304,576]{1,0:T(8,128)(2,1)} %constant_dynamic-update-slice_fusion.12), kind=kOutput, calls=%fused_computation.88 | convolution fusion | flops 5435817984 | bytes 16809984 | tf_op jit(solution)/shard_map/dot_general | solution.py:175
  252.8 25.3 %convolution_convert_fusion = bf16[2048,2304]{1,0:T(8,128)(2,1)} fusion(bf16[576,2304]{0,1:T(8,128)(2,1)} %bitcast.23, f32[2048,576]{0,1:T(8,128)} %fusion.51, bf16[2048,2304]{1,0:T(8,128)(2,1)} %all-gather.2.cloned.1.call-done, bf16[2304,576]{1,0:T(8,128)(2,1)} %constant_dynamic-update-slice_fusion.5), kind=kOutput, calls=%fused_computation | convolution fusion | flops 10888151040 | bytes 28901376 | tf_op jit(solution)/shard_map/dot_general | solution.py:178
  279.8 110.1 %reduce-scatter.2.cloned.1.call-done = bf16[128,2304]{1,0:T(8,128)(2,1)} async-done(((bf16[2048,2304]{1,0:T(8,128)(2,1)}), bf16[128,2304]{1,0:T(8,128)(2,1)}) %reduce-scatter.2.cloned.1.call-update) | async-done | bytes 589840 | tf_op jit(solution)/shard_map/reduce_scatter | solution.py:179
  391.1 2.2 fusion.26
  (92 shorter events, 55.2 us)
Async XLA Ops:
  6.5 235.6 %all-gather.2.cloned.1.call-start = ((), (), s32[]{:S(2)}) async-start(), calls=%async_computation.1 | async-start | bytes 10027008 | tf_op jit(solution)/shard_map/all_gather | solution.py:174
  33.2 13.9 %collective-permute-start = (bf16[128,2304]{1,0:T(8,128)(2,1)}, bf16[128,2304]{1,0:T(8,128)(2,1)}, u32[]{:S(2)}, u32[]{:S(2)}) collective-permute-start(bf16[128,2304]{1,0:T(8,128)(2,1)} %constant_dynamic-slice_fusion.4), channel_id=1, source_target_pairs={{0,2},{2,0},{1,3},{3,1},{4,6},{6,4},{5,7},{7,5},{8,10},{10,8},{9,1... | collective-permute-start | bytes 1769480 | tf_op jit(solution)/shard_map/ppermute | solution.py:165
  51.9 337.9 %reduce-scatter.2.cloned.1.call-start = ((), (), s32[]{:S(2)}) async-start(), calls=%async_computation.2 | async-start | bytes 10027008 | tf_op jit(solution)/shard_map/reduce_scatter | solution.py:179
  54.9 57.0 %collective-permute-start.2 = (bf16[288,576]{1,0:T(8,128)(2,1)}, bf16[288,576]{1,0:T(8,128)(2,1)}, u32[]{:S(2)}, u32[]{:S(2)}) collective-permute-start(bf16[288,576]{1,0:T(8,128)(2,1)} %get-tuple-element.8), channel_id=1, source_target_pairs={{0,4},{4,0},{8,12},{12,8},{1,5},{5,1},{9,13},{13,9},{2,6},{6,2},{1... | collective-permute-start | bytes 995336 | tf_op jit(solution)/shard_map/ppermute | solution.py:51
  57.6 56.6 %collective-permute-start.8 = (bf16[288,576]{1,0:T(8,128)(2,1)}, bf16[288,576]{1,0:T(8,128)(2,1)}, u32[]{:S(2)}, u32[]{:S(2)}) collective-permute-start(bf16[288,576]{1,0:T(8,128)(2,1)} %get-tuple-element.11), channel_id=1, source_target_pairs={{0,4},{4,0},{8,12},{12,8},{1,5},{5,1},{9,13},{13,9},{2,6},{6,2},{1... | collective-permute-start | bytes 995336 | tf_op jit(solution)/shard_map/ppermute | solution.py:51
  62.7 46.0 %collective-permute-start.14 = (bf16[288,576]{1,0:T(8,128)(2,1)}, bf16[288,576]{1,0:T(8,128)(2,1)}, u32[]{:S(2)}, u32[]{:S(2)}) collective-permute-start(bf16[288,576]{1,0:T(8,128)(2,1)} %copy.47), channel_id=1, source_target_pairs={{0,4},{4,0},{8,12},{12,8},{1,5},{5,1},{9,13},{13,9},{2,6},{6,2},{1... | collective-permute-start | bytes 995336 | tf_op jit(solution)/shard_map/ppermute | solution.py:51
  63.7 50.9 %collective-permute-start.16 = (bf16[288,576]{1,0:T(8,128)(2,1)}, bf16[288,576]{1,0:T(8,128)(2,1)}, u32[]{:S(2)}, u32[]{:S(2)}) collective-permute-start(bf16[288,576]{1,0:T(8,128)(2,1)} %copy.48), channel_id=1, source_target_pairs={{0,8},{4,12},{8,0},{12,4},{1,9},{5,13},{9,1},{13,5},{2,10},{6,14},... | collective-permute-start | bytes 995336 | tf_op jit(solution)/shard_map/ppermute | solution.py:51
  67.1 56.8 %collective-permute-start.18 = (bf16[288,576]{1,0:T(8,128)(2,1)}, bf16[288,576]{1,0:T(8,128)(2,1)}, u32[]{:S(2)}, u32[]{:S(2)}) collective-permute-start(bf16[288,576]{1,0:T(8,128)(2,1)} %copy.49), channel_id=1, source_target_pairs={{0,12},{4,8},{8,4},{12,0},{1,13},{5,9},{9,5},{13,1},{2,14},{6,10},... | collective-permute-start | bytes 995336 | tf_op jit(solution)/shard_map/ppermute | solution.py:51
  79.4 34.9 %copy-start.6 = (bf16[288,576]{1,0:T(8,128)(2,1)S(1)}, bf16[288,576]{1,0:T(8,128)(2,1)}, u32[]{:S(2)}) copy-start(bf16[288,576]{1,0:T(8,128)(2,1)} %get-tuple-element.9) | copy-start | bytes 995332
  108.6 17.9 %collective-permute-start.15 = (bf16[288,576]{1,0:T(8,128)(2,1)}, bf16[288,576]{1,0:T(8,128)(2,1)S(1)}, u32[]{:S(2)}, u32[]{:S(2)}) collective-permute-start(bf16[288,576]{1,0:T(8,128)(2,1)} %collective-permute-done.14), channel_id=1, source_target_pairs={{0,16},{16,0},{1,17},{17,1},{2,18},{18,2},{3,19},{19,3},{4,20},{20... | collective-permute-start | bytes 995336 | tf_op jit(solution)/shard_map/ppermute | solution.py:52
  111.9 87.0 %collective-permute-start.6 = (bf16[288,576]{1,0:T(8,128)(2,1)S(1)}, bf16[288,576]{1,0:T(8,128)(2,1)S(1)}, u32[]{:S(2)}, u32[]{:S(2)}) collective-permute-start(bf16[288,576]{1,0:T(8,128)(2,1)S(1)} %copy-done.5), channel_id=1, source_target_pairs={{0,12},{4,8},{8,4},{12,0},{1,13},{5,9},{9,5},{13,1},{2,14},{6,10},... | collective-permute-start | bytes 995336 | tf_op jit(solution)/shard_map/ppermute | solution.py:51
  114.2 74.8 %collective-permute-start.4 = (bf16[288,576]{1,0:T(8,128)(2,1)S(1)}, bf16[288,576]{1,0:T(8,128)(2,1)}, u32[]{:S(2)}, u32[]{:S(2)}) collective-permute-start(bf16[288,576]{1,0:T(8,128)(2,1)S(1)} %copy-done.6), channel_id=1, source_target_pairs={{0,8},{4,12},{8,0},{12,4},{1,9},{5,13},{9,1},{13,5},{2,10},{6,14},... | collective-permute-start | bytes 995336 | tf_op jit(solution)/shard_map/ppermute | solution.py:51
  114.6 74.4 %collective-permute-start.17 = (bf16[288,576]{1,0:T(8,128)(2,1)}, bf16[288,576]{1,0:T(8,128)(2,1)S(1)}, u32[]{:S(2)}, u32[]{:S(2)}) collective-permute-start(bf16[288,576]{1,0:T(8,128)(2,1)} %collective-permute-done.16), channel_id=1, source_target_pairs={{0,16},{16,0},{1,17},{17,1},{2,18},{18,2},{3,19},{19,3},{4,20},{20... | collective-permute-start | bytes 995336 | tf_op jit(solution)/shard_map/ppermute | solution.py:52
  123.9 76.4 %collective-permute-start.12 = (bf16[288,576]{1,0:T(8,128)(2,1)S(1)}, bf16[288,576]{1,0:T(8,128)(2,1)S(1)}, u32[]{:S(2)}, u32[]{:S(2)}) collective-permute-start(bf16[288,576]{1,0:T(8,128)(2,1)S(1)} %get-tuple-element.10), channel_id=1, source_target_pairs={{0,12},{4,8},{8,4},{12,0},{1,13},{5,9},{9,5},{13,1},{2,14},{6,10},... | collective-permute-start | bytes 995336 | tf_op jit(solution)/shard_map/ppermute | solution.py:51
  126.5 66.4 %collective-permute-start.19 = (bf16[288,576]{1,0:T(8,128)(2,1)}, bf16[288,576]{1,0:T(8,128)(2,1)S(1)}, u32[]{:S(2)}, u32[]{:S(2)}) collective-permute-start(bf16[288,576]{1,0:T(8,128)(2,1)} %collective-permute-done.18), channel_id=1, source_target_pairs={{0,16},{16,0},{1,17},{17,1},{2,18},{18,2},{3,19},{19,3},{4,20},{20... | collective-permute-start | bytes 995336 | tf_op jit(solution)/shard_map/ppermute | solution.py:52
  189.0 26.5 %collective-permute-start.10 = (bf16[288,576]{1,0:T(8,128)(2,1)S(1)}, bf16[288,576]{1,0:T(8,128)(2,1)S(1)}, u32[]{:S(2)}, u32[]{:S(2)}) collective-permute-start(bf16[288,576]{1,0:T(8,128)(2,1)S(1)} %get-tuple-element.12), channel_id=1, source_target_pairs={{0,8},{4,12},{8,0},{12,4},{1,9},{5,13},{9,1},{13,5},{2,10},{6,14},... | collective-permute-start | bytes 995336 | tf_op jit(solution)/shard_map/ppermute | solution.py:51
  189.0 28.0 %collective-permute-start.3 = (bf16[288,576]{1,0:T(8,128)(2,1)}, bf16[288,576]{1,0:T(8,128)(2,1)}, u32[]{:S(2)}, u32[]{:S(2)}) collective-permute-start(bf16[288,576]{1,0:T(8,128)(2,1)} %collective-permute-done.2), channel_id=1, source_target_pairs={{0,16},{16,0},{1,17},{17,1},{2,18},{18,2},{3,19},{19,3},{4,20},{20... | collective-permute-start | bytes 995336 | tf_op jit(solution)/shard_map/ppermute | solution.py:52
  192.9 28.2 %collective-permute-start.5 = (bf16[288,576]{1,0:T(8,128)(2,1)}, bf16[288,576]{1,0:T(8,128)(2,1)}, u32[]{:S(2)}, u32[]{:S(2)}) collective-permute-start(bf16[288,576]{1,0:T(8,128)(2,1)} %collective-permute-done.4), channel_id=1, source_target_pairs={{0,16},{16,0},{1,17},{17,1},{2,18},{18,2},{3,19},{19,3},{4,20},{20... | collective-permute-start | bytes 995336 | tf_op jit(solution)/shard_map/ppermute | solution.py:52
  198.9 24.7 %collective-permute-start.9 = (bf16[288,576]{1,0:T(8,128)(2,1)}, bf16[288,576]{1,0:T(8,128)(2,1)S(1)}, u32[]{:S(2)}, u32[]{:S(2)}) collective-permute-start(bf16[288,576]{1,0:T(8,128)(2,1)} %collective-permute-done.8), channel_id=1, source_target_pairs={{0,16},{16,0},{1,17},{17,1},{2,18},{18,2},{3,19},{19,3},{4,20},{20... | collective-permute-start | bytes 995336 | tf_op jit(solution)/shard_map/ppermute | solution.py:52
  200.3 40.3 %collective-permute-start.7 = (bf16[288,576]{1,0:T(8,128)(2,1)S(1)}, bf16[288,576]{1,0:T(8,128)(2,1)S(1)}, u32[]{:S(2)}, u32[]{:S(2)}) collective-permute-start(bf16[288,576]{1,0:T(8,128)(2,1)S(1)} %collective-permute-done.6), channel_id=1, source_target_pairs={{0,16},{16,0},{1,17},{17,1},{2,18},{18,2},{3,19},{19,3},{4,20},{20... | collective-permute-start | bytes 995336 | tf_op jit(solution)/shard_map/ppermute | solution.py:52
  215.5 25.8 %collective-permute-start.13 = (bf16[288,576]{1,0:T(8,128)(2,1)S(1)}, bf16[288,576]{1,0:T(8,128)(2,1)S(1)}, u32[]{:S(2)}, u32[]{:S(2)}) collective-permute-start(bf16[288,576]{1,0:T(8,128)(2,1)S(1)} %collective-permute-done.12), channel_id=1, source_target_pairs={{0,16},{16,0},{1,17},{17,1},{2,18},{18,2},{3,19},{19,3},{4,20},{20... | collective-permute-start | bytes 995336 | tf_op jit(solution)/shard_map/ppermute | solution.py:52
  217.0 22.0 %collective-permute-start.11 = (bf16[288,576]{1,0:T(8,128)(2,1)S(1)}, bf16[288,576]{1,0:T(8,128)(2,1)S(1)}, u32[]{:S(2)}, u32[]{:S(2)}) collective-permute-start(bf16[288,576]{1,0:T(8,128)(2,1)S(1)} %collective-permute-done.10), channel_id=1, source_target_pairs={{0,16},{16,0},{1,17},{17,1},{2,18},{18,2},{3,19},{19,3},{4,20},{20... | collective-permute-start | bytes 995336 | tf_op jit(solution)/shard_map/ppermute | solution.py:52
  278.0 113.1 %copy-start.9 = (f32[2304]{0:T(1024)S(1)}, f32[2304]{0:T(1024)}, u32[]{:S(2)}) copy-start(f32[2304]{0:T(1024)} %param.23) | copy-start | bytes 27652
  279.1 112.0 %collective-permute-start.1 = (bf16[128,2304]{1,0:T(8,128)(2,1)S(1)}, bf16[128,2304]{1,0:T(8,128)(2,1)S(1)}, u32[]{:S(2)}, u32[]{:S(2)}) collective-permute-start(bf16[128,2304]{1,0:T(8,128)(2,1)S(1)} %copy-done.3), channel_id=1, source_target_pairs={{0,0},{1,2},{2,1},{3,3},{4,4},{5,6},{6,5},{7,7},{8,8},{9,10},{10,9... | collective-permute-start | bytes 1769480 | tf_op jit(solution)/shard_map/ppermute | solution.py:173
  (8 other events, 111.5 us)
Sparse Core Ops, SparseCore 0:
  52.0 152.7 all-gather.1
  278.2 111.6 reduce-scatter.1

commit v4 on v3

--- a/solution.py
+++ b/solution.py
@@ -176,8 +176,13 @@
     up_part = jnp.dot(ffn_rows, up_mine, preferred_element_type=jnp.float32)
     hidden = (jax.nn.gelu(gate, approximate=True) * up_part).astype(jnp.bfloat16)
     terms = jnp.dot(hidden, down_mine, preferred_element_type=jnp.float32).astype(jnp.bfloat16)
+    by_section = terms.reshape(-1, section_size, out_rows, terms.shape[1])
+    kept_terms = lax.dynamic_index_in_dim(by_section, section_index, 1, keepdims=False)
+    sent_terms = lax.dynamic_index_in_dim(by_section, 1 - section_index, 1, keepdims=False)
+    came_terms = lax.ppermute(sent_terms, "section", swap)
+    chip_sum = (kept_terms.astype(jnp.float32) + came_terms.astype(jnp.float32)).astype(jnp.bfloat16)
     ffn_out = lax.psum_scatter(
-        terms, ("blk", "heads", "section"), scatter_dimension=0, tiled=True
+        chip_sum.reshape(-1, terms.shape[1]), ("blk", "heads"), scatter_dimension=0, tiled=True
     ).astype(jnp.float32)
     return (residual_out.astype(jnp.float32) + rms_scale(ffn_out, post_ffn_gain)).astype(
         jnp.bfloat16

time: 401 us -> 392 us (0.978)
  waiting for transfers between devices: 243 us -> 234 us
  other arithmetic: 9.93 us -> 15 us
  local copies, waits for them, and re-layouts: 53.7 us -> 48.9 us
    reduce_scatter x1, waiting for transfers between devices: 110 us -> 93 us  [rows_body(): lax.psum_scatter(chip_sum.reshape(-1, terms.shape[1]), ('blk', 'heads'),...]
    ppermute x0 -> x1, waiting for transfers between devices: none -> 8.25 us  [rows_body(): came_terms = lax.ppermute(sent_terms, 'section', swap)]
    convert_element_type x0 -> x1, other arithmetic: none -> 7.03 us  [rows_body(): (kept_terms.astype(jnp.float32) + came_terms.astype(jnp.float32)).astype(...]
    squeeze x0 -> x1, local copies, waits for them, and re-layouts: none -> 4.78 us  [rows_body(): lax.dynamic_index_in_dim(by_section, 1 - section_index, 1, keepdims=False)]
  transfers between devices with their start and end apart: 22 -> 23, of which waited for: 7 -> 9; matrix products, arithmetic and copies ran while one was open for 13% -> 11% of each run, Pallas kernels for 0% -> 0%
where the time goes in v4:
time: 392 us; the launch traced here: 391 us
  waiting for transfers between devices  234 us (60%)
  local copies, waits for them, and re-layouts  48.9 us (12%)
  matrix products  39.9 us (10%)
  starting transfers between devices  22.4 us (6%)
  blocking collectives  17.4 us (4%)
  other arithmetic  15 us (4%)
  between operations  13.7 us (3%)
    ppermute x9, waiting for transfers between devices, reshard_over_blk(): first = lax.ppermute(packet, 'blk', [(i, i ^ step) for i in range(count)])  110 us
    reduce_scatter x1, waiting for transfers between devices, rows_body(): lax.psum_scatter(chip_sum.reshape(-1, terms.shape[1]), ('blk', 'heads'),...  93 us
    dot_general x1, matrix products, rows_body(): jnp.dot(hidden, down_mine, preferred_element_type=jnp.float32)  25.3 us
    dynamic_update_slice x18, local copies, waits for them, and re-layouts, reshard_over_blk(): lax.dynamic_update_slice_in_dim(whole, part, peer * sizes[0] + group * ha...  19.2 us
    all_gather x1, blocking collectives, rows_body(): lax.all_gather(jnp.stack([keys_local, values_local]), 'blk', axis=1, tile...  17.4 us
    ppermute x1, waiting for transfers between devices, rows_body(): other_term = lax.ppermute(sent_term, 'heads', swap)  12.1 us
    ppermute x9, waiting for transfers between devices, reshard_over_blk(): second = lax.ppermute(first, 'groups', [(0, 1), (1, 0)])  10.6 us
    ppermute x9, starting transfers between devices, reshard_over_blk(): first = lax.ppermute(packet, 'blk', [(i, i ^ step) for i in range(count)])  10.1 us
  transfers between devices with their start and end apart: 23, of which 9 were waited for; matrix products, arithmetic and copies ran while one was open for 11% of the time, Pallas kernels for 0%

profile of v4, /device:TPU:0, one launch (start us, length us, event | category | flops | bytes accessed | tf_op | source)
XLA Modules:
  0.0 391.3 jit_solution(4981573007292923388)
XLA Ops:
  7.5 17.4 %all_gather.6 = bf16[2,512,256]{2,1,0:T(8,128)(2,1)S(1)} all-gather(bf16[2,128,256]{2,1,0:T(8,128)(2,1)S(1)} %pad_maximum_fusion), channel_id=1, replica_groups=mesh['groups'=2,'blk'=4,'heads'=2,'section'=2] {'blk'}, dimensions={1}, use_global_device_ids=true | all-gather | bytes 655360 | tf_op jit(solution)/shard_map/all_gather | solution.py:146
  26.7 3.2 fusion.47
  33.3 12.1 %collective-permute-done = bf16[128,2304]{1,0:T(8,128)(2,1)S(1)} collective-permute-done((bf16[128,2304]{1,0:T(8,128)(2,1)S(1)}, bf16[128,2304]{1,0:T(8,128)(2,1)S(1)}, u32[]{:S(2)}, u32[]{:S(2)}) %collective-permute-start) | collective-permute-done | bytes 589856 | tf_op jit(solution)/shard_map/ppermute | solution.py:165
  48.2 3.0 fusion.45
  51.2 2.8 fusion.46
  54.0 2.0 collective-permute-start.8
  56.0 2.2 constant_dynamic-slice_fusion
  60.0 2.5 collective-permute-start.16
  71.7 2.5 dynamic-slice_dynamic-update-slice_fusion
  74.5 30.3 %collective-permute-done.14 = bf16[288,576]{1,0:T(8,128)(2,1)} collective-permute-done((bf16[288,576]{1,0:T(8,128)(2,1)}, bf16[288,576]{1,0:T(8,128)(2,1)}, u32[]{:S(2)}, u32[]{:S(2)}) %collective-permute-start.14) | collective-permute-done | bytes 331808 | tf_op jit(solution)/shard_map/ppermute | solution.py:51
  112.8 7.4 %collective-permute-done.18 = bf16[288,576]{1,0:T(8,128)(2,1)} collective-permute-done((bf16[288,576]{1,0:T(8,128)(2,1)}, bf16[288,576]{1,0:T(8,128)(2,1)}, u32[]{:S(2)}, u32[]{:S(2)}) %collective-permute-start.18) | collective-permute-done | bytes 331808 | tf_op jit(solution)/shard_map/ppermute | solution.py:51
  122.8 40.5 %collective-permute-done.4 = bf16[288,576]{1,0:T(8,128)(2,1)} collective-permute-done((bf16[288,576]{1,0:T(8,128)(2,1)S(1)}, bf16[288,576]{1,0:T(8,128)(2,1)}, u32[]{:S(2)}, u32[]{:S(2)}) %collective-permute-start.4) | collective-permute-done | bytes 331808 | tf_op jit(solution)/shard_map/ppermute | solution.py:51
  168.4 3.1 copy.47
  172.4 31.7 %collective-permute-done.10 = bf16[288,576]{1,0:T(8,128)(2,1)} collective-permute-done((bf16[288,576]{1,0:T(8,128)(2,1)}, bf16[288,576]{1,0:T(8,128)(2,1)}, u32[]{:S(2)}, u32[]{:S(2)}) %collective-permute-start.10) | collective-permute-done | bytes 331808 | tf_op jit(solution)/shard_map/ppermute | solution.py:51
  215.3 2.0 constant_dynamic-update-slice_fusion.10
  217.3 6.4 %collective-permute-done.11 = bf16[288,576]{1,0:T(8,128)(2,1)S(1)} collective-permute-done((bf16[288,576]{1,0:T(8,128)(2,1)}, bf16[288,576]{1,0:T(8,128)(2,1)S(1)}, u32[]{:S(2)}, u32[]{:S(2)}) %collective-permute-start.11) | collective-permute-done | bytes 331808 | tf_op jit(solution)/shard_map/ppermute | solution.py:52
  226.3 4.2 %collective-permute-done.13 = bf16[288,576]{1,0:T(8,128)(2,1)S(1)} collective-permute-done((bf16[288,576]{1,0:T(8,128)(2,1)}, bf16[288,576]{1,0:T(8,128)(2,1)S(1)}, u32[]{:S(2)}, u32[]{:S(2)}) %collective-permute-start.13) | collective-permute-done | bytes 331808 | tf_op jit(solution)/shard_map/ppermute | solution.py:52
  231.3 9.7 %fusion.52 = f32[2048,576]{0,1:T(8,128)} fusion(bf16[2048,2304]{1,0:T(8,128)(2,1)} %all-gather.2.cloned.1.call-done, bf16[2304,576]{1,0:T(8,128)(2,1)S(1)} %constant_dynamic-update-slice_fusion.13), kind=kOutput, calls=%fused_computation.91 | convolution fusion | flops 5435817984 | bytes 16809984 | tf_op jit(solution)/shard_map/dot_general | solution.py:175
  240.9 25.3 %convolution_convert_fusion = bf16[2048,2304]{1,0:T(8,128)(2,1)} fusion(bf16[576,2304]{0,1:T(8,128)(2,1)} %bitcast.36, f32[2048,576]{0,1:T(8,128)} %fusion.52, bf16[2048,2304]{1,0:T(8,128)(2,1)} %all-gather.2.cloned.1.call-done, bf16[2304,576]{1,0:T(8,128)(2,1)} %constant_dynamic-update-slice_fusion.7), kind=kOutput, calls=%fused_computation | convolution fusion | flops 10888151040 | bytes 28901376 | tf_op jit(solution)/shard_map/dot_general | solution.py:178
  266.2 4.8 %dynamic-slice_bitcast_fusion = bf16[8,128,2304]{2,1,0:T(8,128)(2,1)} fusion(bf16[8,2,128,2304]{3,2,1,0:T(8,128)(2,1)} %bitcast.34, s32[]{:T(128)S(6)} %select_n.110), kind=kLoop, calls=%fused_computation.13 | loop fusion | bytes 9437188 | tf_op jit(solution)/shard_map/jit(dynamic_index_in_dim)/squeeze | solution.py:181
  271.0 8.2 %collective-permute-done.20 = bf16[8,128,2304]{2,1,0:T(8,128)(2,1)} collective-permute-done((bf16[8,128,2304]{2,1,0:T(8,128)(2,1)}, bf16[8,128,2304]{2,1,0:T(8,128)(2,1)}, u32[]{:S(2)}, u32[]{:S(2)}) %collective-permute-start.20) | collective-permute-done | bytes 4718624 | tf_op jit(solution)/shard_map/ppermute | solution.py:182
  279.2 7.0 %fusion = bf16[8,128,2304]{2,1,0:T(8,128)(2,1)} fusion(bf16[8,128,2304]{2,1,0:T(8,128)(2,1)} %collective-permute-done.20, bf16[8,2,128,2304]{3,2,1,0:T(8,128)(2,1)} %bitcast.35, s32[]{:T(128)S(6)} %select_n.109), kind=kLoop, calls=%fused_computation.2 | loop fusion | flops 9437184 | bytes 14155780 | tf_op jit(solution)/shard_map/convert_element_type | solution.py:183
  288.0 93.0 %reduce-scatter.2.cloned.1.call-done = bf16[128,2304]{1,0:T(8,128)(2,1)} async-done(((bf16[1024,2304]{1,0:T(8,128)(2,1)}), bf16[128,2304]{1,0:T(8,128)(2,1)}) %reduce-scatter.2.cloned.1.call-update) | async-done | bytes 589840 | tf_op jit(solution)/shard_map/reduce_scatter | solution.py:184
  382.3 2.2 fusion.27
  (102 shorter events, 54.3 us)
Async XLA Ops:
  6.5 224.7 %all-gather.2.cloned.1.call-start = ((), (), s32[]{:S(2)}) async-start(), calls=%async_computation.1 | async-start | bytes 10027008 | tf_op jit(solution)/shard_map/all_gather | solution.py:174
  31.8 13.7 %collective-permute-start = (bf16[128,2304]{1,0:T(8,128)(2,1)S(1)}, bf16[128,2304]{1,0:T(8,128)(2,1)S(1)}, u32[]{:S(2)}, u32[]{:S(2)}) collective-permute-start(bf16[128,2304]{1,0:T(8,128)(2,1)S(1)} %constant_dynamic-slice_fusion.4), channel_id=1, source_target_pairs={{0,2},{2,0},{1,3},{3,1},{4,6},{6,4},{5,7},{7,5},{8,10},{10,8},{9,1... | collective-permute-start | bytes 1769480 | tf_op jit(solution)/shard_map/ppermute | solution.py:165
  48.1 332.9 %reduce-scatter.2.cloned.1.call-start = ((), (), s32[]{:S(2)}) async-start(), calls=%async_computation.2 | async-start | bytes 5308416 | tf_op jit(solution)/shard_map/reduce_scatter | solution.py:184
  51.2 56.2 %collective-permute-start.2 = (bf16[288,576]{1,0:T(8,128)(2,1)}, bf16[288,576]{1,0:T(8,128)(2,1)}, u32[]{:S(2)}, u32[]{:S(2)}) collective-permute-start(bf16[288,576]{1,0:T(8,128)(2,1)} %get-tuple-element.8), channel_id=1, source_target_pairs={{0,4},{4,0},{8,12},{12,8},{1,5},{5,1},{9,13},{13,9},{2,6},{6,2},{1... | collective-permute-start | bytes 995336 | tf_op jit(solution)/shard_map/ppermute | solution.py:51
  54.0 54.5 %collective-permute-start.8 = (bf16[288,576]{1,0:T(8,128)(2,1)}, bf16[288,576]{1,0:T(8,128)(2,1)}, u32[]{:S(2)}, u32[]{:S(2)}) collective-permute-start(bf16[288,576]{1,0:T(8,128)(2,1)} %get-tuple-element.11), channel_id=1, source_target_pairs={{0,4},{4,0},{8,12},{12,8},{1,5},{5,1},{9,13},{13,9},{2,6},{6,2},{1... | collective-permute-start | bytes 995336 | tf_op jit(solution)/shard_map/ppermute | solution.py:51
  59.1 45.7 %collective-permute-start.14 = (bf16[288,576]{1,0:T(8,128)(2,1)}, bf16[288,576]{1,0:T(8,128)(2,1)}, u32[]{:S(2)}, u32[]{:S(2)}) collective-permute-start(bf16[288,576]{1,0:T(8,128)(2,1)} %copy.50), channel_id=1, source_target_pairs={{0,4},{4,0},{8,12},{12,8},{1,5},{5,1},{9,13},{13,9},{2,6},{6,2},{1... | collective-permute-start | bytes 995336 | tf_op jit(solution)/shard_map/ppermute | solution.py:51
  60.0 50.3 %collective-permute-start.16 = (bf16[288,576]{1,0:T(8,128)(2,1)}, bf16[288,576]{1,0:T(8,128)(2,1)}, u32[]{:S(2)}, u32[]{:S(2)}) collective-permute-start(bf16[288,576]{1,0:T(8,128)(2,1)} %copy.51), channel_id=1, source_target_pairs={{0,8},{4,12},{8,0},{12,4},{1,9},{5,13},{9,1},{13,5},{2,10},{6,14},... | collective-permute-start | bytes 995336 | tf_op jit(solution)/shard_map/ppermute | solution.py:51
  63.5 56.7 %collective-permute-start.18 = (bf16[288,576]{1,0:T(8,128)(2,1)}, bf16[288,576]{1,0:T(8,128)(2,1)}, u32[]{:S(2)}, u32[]{:S(2)}) collective-permute-start(bf16[288,576]{1,0:T(8,128)(2,1)} %copy.52), channel_id=1, source_target_pairs={{0,12},{4,8},{8,4},{12,0},{1,13},{5,9},{9,5},{13,1},{2,14},{6,10},... | collective-permute-start | bytes 995336 | tf_op jit(solution)/shard_map/ppermute | solution.py:51
  104.8 15.3 %collective-permute-start.15 = (bf16[288,576]{1,0:T(8,128)(2,1)}, bf16[288,576]{1,0:T(8,128)(2,1)S(1)}, u32[]{:S(2)}, u32[]{:S(2)}) collective-permute-start(bf16[288,576]{1,0:T(8,128)(2,1)} %collective-permute-done.14), channel_id=1, source_target_pairs={{0,16},{16,0},{1,17},{17,1},{2,18},{18,2},{3,19},{19,3},{4,20},{20... | collective-permute-start | bytes 995336 | tf_op jit(solution)/shard_map/ppermute | solution.py:52
  107.4 55.9 %collective-permute-start.4 = (bf16[288,576]{1,0:T(8,128)(2,1)S(1)}, bf16[288,576]{1,0:T(8,128)(2,1)}, u32[]{:S(2)}, u32[]{:S(2)}) collective-permute-start(bf16[288,576]{1,0:T(8,128)(2,1)S(1)} %copy-done.9), channel_id=1, source_target_pairs={{0,8},{4,12},{8,0},{12,4},{1,9},{5,13},{9,1},{13,5},{2,10},{6,14},... | collective-permute-start | bytes 995336 | tf_op jit(solution)/shard_map/ppermute | solution.py:51
  108.5 63.0 %collective-permute-start.6 = (bf16[288,576]{1,0:T(8,128)(2,1)}, bf16[288,576]{1,0:T(8,128)(2,1)}, u32[]{:S(2)}, u32[]{:S(2)}) collective-permute-start(bf16[288,576]{1,0:T(8,128)(2,1)} %get-tuple-element.7), channel_id=1, source_target_pairs={{0,12},{4,8},{8,4},{12,0},{1,13},{5,9},{9,5},{13,1},{2,14},{6,10},... | collective-permute-start | bytes 995336 | tf_op jit(solution)/shard_map/ppermute | solution.py:51
  110.4 54.8 %collective-permute-start.17 = (bf16[288,576]{1,0:T(8,128)(2,1)}, bf16[288,576]{1,0:T(8,128)(2,1)S(1)}, u32[]{:S(2)}, u32[]{:S(2)}) collective-permute-start(bf16[288,576]{1,0:T(8,128)(2,1)} %collective-permute-done.16), channel_id=1, source_target_pairs={{0,16},{16,0},{1,17},{17,1},{2,18},{18,2},{3,19},{19,3},{4,20},{20... | collective-permute-start | bytes 995336 | tf_op jit(solution)/shard_map/ppermute | solution.py:52
  120.2 83.9 %collective-permute-start.10 = (bf16[288,576]{1,0:T(8,128)(2,1)}, bf16[288,576]{1,0:T(8,128)(2,1)}, u32[]{:S(2)}, u32[]{:S(2)}) collective-permute-start(bf16[288,576]{1,0:T(8,128)(2,1)} %get-tuple-element.12), channel_id=1, source_target_pairs={{0,8},{4,12},{8,0},{12,4},{1,9},{5,13},{9,1},{13,5},{2,10},{6,14},... | collective-permute-start | bytes 995336 | tf_op jit(solution)/shard_map/ppermute | solution.py:51
  120.2 47.0 %collective-permute-start.19 = (bf16[288,576]{1,0:T(8,128)(2,1)}, bf16[288,576]{1,0:T(8,128)(2,1)S(1)}, u32[]{:S(2)}, u32[]{:S(2)}) collective-permute-start(bf16[288,576]{1,0:T(8,128)(2,1)} %collective-permute-done.18), channel_id=1, source_target_pairs={{0,16},{16,0},{1,17},{17,1},{2,18},{18,2},{3,19},{19,3},{4,20},{20... | collective-permute-start | bytes 995336 | tf_op jit(solution)/shard_map/ppermute | solution.py:52
  163.3 42.2 %collective-permute-start.12 = (bf16[288,576]{1,0:T(8,128)(2,1)S(1)}, bf16[288,576]{1,0:T(8,128)(2,1)}, u32[]{:S(2)}, u32[]{:S(2)}) collective-permute-start(bf16[288,576]{1,0:T(8,128)(2,1)S(1)} %get-tuple-element.10), channel_id=1, source_target_pairs={{0,12},{4,8},{8,4},{12,0},{1,13},{5,9},{9,5},{13,1},{2,14},{6,10},... | collective-permute-start | bytes 995336 | tf_op jit(solution)/shard_map/ppermute | solution.py:51
  165.2 41.0 %collective-permute-start.3 = (bf16[288,576]{1,0:T(8,128)(2,1)}, bf16[288,576]{1,0:T(8,128)(2,1)}, u32[]{:S(2)}, u32[]{:S(2)}) collective-permute-start(bf16[288,576]{1,0:T(8,128)(2,1)} %collective-permute-done.2), channel_id=1, source_target_pairs={{0,16},{16,0},{1,17},{17,1},{2,18},{18,2},{3,19},{19,3},{4,20},{20... | collective-permute-start | bytes 995336 | tf_op jit(solution)/shard_map/ppermute | solution.py:52
  167.1 43.9 %collective-permute-start.5 = (bf16[288,576]{1,0:T(8,128)(2,1)}, bf16[288,576]{1,0:T(8,128)(2,1)}, u32[]{:S(2)}, u32[]{:S(2)}) collective-permute-start(bf16[288,576]{1,0:T(8,128)(2,1)} %collective-permute-done.4), channel_id=1, source_target_pairs={{0,16},{16,0},{1,17},{17,1},{2,18},{18,2},{3,19},{19,3},{4,20},{20... | collective-permute-start | bytes 995336 | tf_op jit(solution)/shard_map/ppermute | solution.py:52
  171.5 43.0 %collective-permute-start.9 = (bf16[288,576]{1,0:T(8,128)(2,1)}, bf16[288,576]{1,0:T(8,128)(2,1)S(1)}, u32[]{:S(2)}, u32[]{:S(2)}) collective-permute-start(bf16[288,576]{1,0:T(8,128)(2,1)} %collective-permute-done.8), channel_id=1, source_target_pairs={{0,16},{16,0},{1,17},{17,1},{2,18},{18,2},{3,19},{19,3},{4,20},{20... | collective-permute-start | bytes 995336 | tf_op jit(solution)/shard_map/ppermute | solution.py:52
  204.1 22.1 %collective-permute-start.7 = (bf16[288,576]{1,0:T(8,128)(2,1)}, bf16[288,576]{1,0:T(8,128)(2,1)S(1)}, u32[]{:S(2)}, u32[]{:S(2)}) collective-permute-start(bf16[288,576]{1,0:T(8,128)(2,1)} %collective-permute-done.6), channel_id=1, source_target_pairs={{0,16},{16,0},{1,17},{17,1},{2,18},{18,2},{3,19},{19,3},{4,20},{20... | collective-permute-start | bytes 995336 | tf_op jit(solution)/shard_map/ppermute | solution.py:52
  205.5 18.2 %collective-permute-start.11 = (bf16[288,576]{1,0:T(8,128)(2,1)}, bf16[288,576]{1,0:T(8,128)(2,1)S(1)}, u32[]{:S(2)}, u32[]{:S(2)}) collective-permute-start(bf16[288,576]{1,0:T(8,128)(2,1)} %collective-permute-done.10), channel_id=1, source_target_pairs={{0,16},{16,0},{1,17},{17,1},{2,18},{18,2},{3,19},{19,3},{4,20},{20... | collective-permute-start | bytes 995336 | tf_op jit(solution)/shard_map/ppermute | solution.py:52
  206.1 24.3 %collective-permute-start.13 = (bf16[288,576]{1,0:T(8,128)(2,1)}, bf16[288,576]{1,0:T(8,128)(2,1)S(1)}, u32[]{:S(2)}, u32[]{:S(2)}) collective-permute-start(bf16[288,576]{1,0:T(8,128)(2,1)} %collective-permute-done.12), channel_id=1, source_target_pairs={{0,16},{16,0},{1,17},{17,1},{2,18},{18,2},{3,19},{19,3},{4,20},{20... | collective-permute-start | bytes 995336 | tf_op jit(solution)/shard_map/ppermute | solution.py:52
  271.0 8.3 %collective-permute-start.20 = (bf16[8,128,2304]{2,1,0:T(8,128)(2,1)}, bf16[8,128,2304]{2,1,0:T(8,128)(2,1)}, u32[]{:S(2)}, u32[]{:S(2)}) collective-permute-start(bf16[8,128,2304]{2,1,0:T(8,128)(2,1)} %dynamic-slice_bitcast_fusion), channel_id=1, source_target_pairs={{0,1},{1,0},{2,3},{3,2},{4,5},{5,4},{6,7},{7,6},{8,9},{9,8},{10,11... | collective-permute-start | bytes 14155784 | tf_op jit(solution)/shard_map/ppermute | solution.py:182
  286.3 98.2 %copy-start.1 = (bf16[256,2304]{1,0:T(8,128)(2,1)S(1)}, bf16[256,2304]{1,0:T(8,128)(2,1)}, u32[]{:S(2)}) copy-start(bf16[256,2304]{1,0:T(8,128)(2,1)} %param.17) | copy-start | bytes 3538948
  287.3 94.9 %collective-permute-start.1 = (bf16[128,2304]{1,0:T(8,128)(2,1)S(1)}, bf16[128,2304]{1,0:T(8,128)(2,1)S(1)}, u32[]{:S(2)}, u32[]{:S(2)}) collective-permute-start(bf16[128,2304]{1,0:T(8,128)(2,1)S(1)} %copy-done.7), channel_id=1, source_target_pairs={{0,0},{1,2},{2,1},{3,3},{4,4},{5,6},{6,5},{7,7},{8,8},{9,10},{10,9... | collective-permute-start | bytes 1769480 | tf_op jit(solution)/shard_map/ppermute | solution.py:173
  (12 other events, 276.1 us)
Sparse Core Ops, SparseCore 0:
  48.2 152.6 all-gather.1
  286.4 94.5 reduce-scatter.1
